TPU v7x, 32 devices: a whole 2x2x4 slice. The times are simulated.
32 devices in a mesh: ctx: 16 (over z, y, x), head: 2 (over core).
Axes of the slice: x: 2, y: 2, z: 4, core: 2. Of those that a mesh axis runs over, the one named last changes fastest.
Arguments:
- lin_queries: bfloat16 [4096, 8192], P('ctx', 'head'), may hold values from -6 to 6
- lin_keys: bfloat16 [4096, 8192], P('ctx', 'head'), may hold values from -6 to 6
- lin_values: bfloat16 [4096, 8192], P('ctx', 'head'), may hold values from -21 to 21
- log_decay: float32 [4096, 64], P('ctx', 'head'), may hold values from -1 to 0
- lin_gate: bfloat16 [4096, 8192], P('ctx', 'head'), may hold values from -6 to 6
- norm_gain: float32 [8192], P('head'), may hold values from 0.1 to 1.9
- soft_queries: bfloat16 [4096, 8192], P('ctx', 'head'), may hold values from -6 to 6
- slab_keys: bfloat16 [4096, 1024], P('ctx', 'head'), may hold values from -6 to 6
- slab_values: bfloat16 [4096, 1024], P('ctx', 'head'), may hold values from -6 to 6
- cache_keys: bfloat16 [16384, 1024], P('ctx', 'head'), may hold values from -6 to 6
- cache_values: bfloat16 [16384, 1024], P('ctx', 'head'), may hold values from -6 to 6
- block_lists: int32 [32, 16], replicated, may hold values from 0 to 127, as said below
- live_counts: int32 [32], replicated, may hold values from 2 to 16
Outputs:
- lin_out: bfloat16 [4096, 8192], P('ctx', 'head')
- soft_out: bfloat16 [4096, 8192], P('ctx', 'head')
Inputs may be any that keep to these rules, and one draw needn't show every extreme that they name: `block_lists`: cache block g lies on ctx index g // 8. One list names 16 blocks on 16 different ctx indices, and all lists of the 2 query blocks of one ctx index name at most one block of any one ctx index. Entries from live_counts on are not read.
All inputs are finite; a program needn't handle non-finite values.
Results may differ from a plain program's by a relative error of at most 0.0046.
Values may be sent and summed in bfloat16 or wider, within the bound.
No kernel may reach another device: no remote copies, remote signals or barrier semaphores. Data moves between devices by JAX's collectives and lax.ppermute only.
A program may use at most 192 MiB of HBM per device.

v0:
```python
import math

import jax
import jax.numpy as jnp
from jax import lax
from jax.sharding import PartitionSpec as P

QUERY_HEADS = 64
HD = 128
BLOCK = 128


def entering_2(array, axis, combine, identity):
    count, index = (lax.axis_size(axis), lax.axis_index(axis))
    everything = jax.tree.map(lambda part: lax.all_gather(part, axis), array)
    start = jax.tree.map(
        lambda part, zero: jnp.broadcast_to(jnp.asarray(zero, part.dtype), part.shape),
        array,
        identity,
    )

    def turn(k, before):
        reached = k < index
        new = combine(before, jax.tree.map(lambda part: part[k], everything))
        return jax.tree.map(lambda a, b: jnp.where(reached, a, b), new, before)

    return lax.fori_loop(0, count, turn, start)


def combine_states(earlier, later):
    early_total, early_state = earlier
    late_total, late_state = later
    return (early_total + late_total, jnp.exp(late_total)[:, None, None] * early_state + late_state)


def lightning(lin_queries, lin_keys, lin_values, log_decay, lin_gate, norm_gain):
    tok_rows = lin_queries.shape[0]
    head_count = lin_queries.shape[1] // HD
    act_queries = (
        jax.nn.silu(lin_queries.astype(jnp.float32))
        .astype(jnp.bfloat16)
        .reshape(tok_rows, head_count, HD)
    )
    act_keys = (
        jax.nn.silu(lin_keys.astype(jnp.float32))
        .astype(jnp.bfloat16)
        .reshape(tok_rows, head_count, HD)
    )
    values_here = lin_values.reshape(tok_rows, head_count, HD)
    running = jnp.cumsum(log_decay, axis=0)
    seg_total = running[-1]
    flipped = running.T
    gaps = flipped[:, :, None] - flipped[:, None, :]
    causal = jnp.arange(tok_rows)[:, None] >= jnp.arange(tok_rows)[None, :]
    weight = jnp.where(causal[None], jnp.exp(jnp.minimum(gaps, 0.0)), 0.0)
    scores = jnp.einsum("thd,shd->hts", act_queries, act_keys, preferred_element_type=jnp.float32)
    lin_scores = (scores * weight).astype(jnp.bfloat16)
    intra = jnp.einsum("hts,shd->thd", lin_scores, values_here, preferred_element_type=jnp.float32)
    fade = jnp.exp(seg_total[None, :] - running)
    seg_state = jnp.einsum(
        "shd,she->hde",
        act_keys.astype(jnp.float32) * fade[:, :, None],
        values_here.astype(jnp.float32),
        precision=lax.Precision.HIGHEST,
    )
    empty_total = jnp.zeros((head_count,), jnp.float32)
    empty_state = jnp.zeros((head_count, HD, HD), jnp.float32)
    unused, entering = entering_2(
        (seg_total, seg_state), "ctx", combine_states, (empty_total, empty_state)
    )
    inter = jnp.exp(running)[:, :, None] * jnp.einsum(
        "thd,hde->the", act_queries.astype(jnp.float32), entering, precision=lax.Precision.HIGHEST
    )
    lin_attn = (intra + inter).reshape(tok_rows, head_count * HD)
    partial_squares = jnp.sum(lin_attn * lin_attn, axis=1)
    whole_squares = lax.psum(partial_squares, "head")
    scaling = lax.rsqrt(whole_squares / (QUERY_HEADS * HD) + 1e-06)
    gated = (
        lin_attn
        * scaling[:, None]
        * norm_gain[None, :]
        * jax.nn.sigmoid(lin_gate.astype(jnp.float32))
    )
    return gated.astype(jnp.bfloat16)


def cache_attention(
    soft_queries, slab_keys, slab_values, cache_keys, cache_values, block_lists, live_counts
):
    tok_rows = soft_queries.shape[0]
    blocks_here = tok_rows // BLOCK
    kv_count = cache_keys.shape[1] // HD
    group_size = soft_queries.shape[1] // HD // kv_count
    ctx_devices = lax.axis_size("ctx")
    my_place = lax.axis_index("ctx")
    stored = cache_keys.shape[0] // BLOCK
    selected = block_lists.shape[1]
    packed = jnp.concatenate(
        [
            cache_keys.reshape(stored, BLOCK, kv_count, HD),
            cache_values.reshape(stored, BLOCK, kv_count, HD),
        ],
        axis=3,
    )
    packed = packed.reshape(stored, BLOCK * kv_count * 2 * HD)
    owner_of = block_lists // stored
    spot_of = block_lists % stored
    matches = (spot_of[:, :, None] == jnp.arange(stored, dtype=jnp.int32)[None, None, :]) & (
        owner_of == my_place
    )[:, :, None]
    my_owners = lax.dynamic_slice_in_dim(owner_of, my_place * blocks_here, blocks_here, 0)
    my_counts = lax.dynamic_slice_in_dim(live_counts, my_place * blocks_here, blocks_here, 0)
    wanted = jnp.any(matches, axis=1)
    outgoing = jnp.dot(
        wanted.astype(jnp.bfloat16), packed, preferred_element_type=jnp.float32
    ).astype(jnp.bfloat16)
    outgoing = outgoing.reshape(ctx_devices, blocks_here, BLOCK, kv_count, 2 * HD)
    arrived = lax.all_to_all(outgoing, "ctx", split_axis=0, concat_axis=0, tiled=True)
    fetched = [arrived[my_owners[block_index], block_index] for block_index in range(blocks_here)]
    local_keys = slab_keys.reshape(tok_rows, kv_count, HD)
    local_values = slab_values.reshape(tok_rows, kv_count, HD)
    inverse_root = 1.0 / math.sqrt(HD)
    results = []
    for block_index in range(blocks_here):
        kv_rows = fetched[block_index].reshape(selected * BLOCK, kv_count, 2 * HD)
        all_keys = jnp.concatenate([kv_rows[:, :, :HD], local_keys], axis=0)
        all_values = jnp.concatenate([kv_rows[:, :, HD:], local_values], axis=0)
        queries = soft_queries[block_index * BLOCK : (block_index + 1) * BLOCK].reshape(
            BLOCK, kv_count, group_size, HD
        )
        scores = (
            jnp.einsum("tkgd,skd->kgts", queries, all_keys, preferred_element_type=jnp.float32)
            * inverse_root
        )
        cache_live = jnp.arange(selected * BLOCK) // BLOCK < my_counts[block_index]
        positions = block_index * BLOCK + jnp.arange(BLOCK)
        causal = jnp.arange(tok_rows)[None, :] <= positions[:, None]
        allowed = jnp.concatenate(
            [jnp.broadcast_to(cache_live[None, :], (BLOCK, selected * BLOCK)), causal], axis=1
        )
        scores = jnp.where(allowed[None, None], scores, -1e30)
        highest = jnp.max(scores, axis=3, keepdims=True)
        weights = jnp.exp(scores - highest)
        totals = jnp.sum(weights, axis=3)
        mixed = jnp.einsum(
            "kgts,skd->tkgd",
            weights.astype(jnp.bfloat16),
            all_values,
            preferred_element_type=jnp.float32,
        )
        normed = mixed / jnp.transpose(totals, (2, 0, 1))[:, :, :, None]
        results.append(normed.astype(jnp.bfloat16).reshape(BLOCK, kv_count * group_size * HD))
    return jnp.concatenate(results, axis=0)


def local(
    lin_queries,
    lin_keys,
    lin_values,
    log_decay,
    lin_gate,
    norm_gain,
    soft_queries,
    slab_keys,
    slab_values,
    cache_keys,
    cache_values,
    block_lists,
    live_counts,
):
    lin_out = lightning(lin_queries, lin_keys, lin_values, log_decay, lin_gate, norm_gain)
    soft_out = cache_attention(
        soft_queries, slab_keys, slab_values, cache_keys, cache_values, block_lists, live_counts
    )
    return (lin_out, soft_out)


def solution(mesh):
    in_specs = (
        P("ctx", "head"),
        P("ctx", "head"),
        P("ctx", "head"),
        P("ctx", "head"),
        P("ctx", "head"),
        P("head"),
        P("ctx", "head"),
        P("ctx", "head"),
        P("ctx", "head"),
        P("ctx", "head"),
        P("ctx", "head"),
        P(),
        P(),
    )
    out_specs = (P("ctx", "head"), P("ctx", "head"))
    return jax.shard_map(local, mesh=mesh, in_specs=in_specs, out_specs=out_specs, check_vma=False)
```

profile of v0, /device:TPU:17, one launch (start us, length us, event | category | flops | bytes accessed | tf_op | source)
XLA Modules:
  0.0 645.6 jit_solution(6744770270289325089)
XLA Ops:
  9.3 4.2 fusion.20
  13.4 4.1 copy.167
  17.5 5.4 fusion.23
  24.3 2.1 reshape.199
  26.4 3.9 pad_maximum_fusion.4
  30.3 4.4 reshape.200
  34.8 7.4 %convolution_convert_fusion = bf16[32,131072]{1,0:T(8,128)(2,1)} fusion(pred[32,8]{0,1:T(8,128)(4,1)S(1)} %fusion.69, bf16[8,131072]{1,0:T(8,128)(2,1)} %reshape.200), kind=kOutput, calls=%fused_computation.5 | convolution fusion | flops 71303168 | bytes 10486016 | tf_op jit(solution)/shard_map/dot_general | solution.py:114
  42.2 11.1 %reshape.201 = bf16[16,2,128,4,256]{4,3,2,1,0:T(4,128)(2,1)} reshape(bf16[32,131072]{1,0:T(8,128)(2,1)} %convolution_convert_fusion) | data formatting | bytes 16777216 | tf_op jit(solution)/shard_map/reshape | solution.py:117
  53.3 6.7 %all-to-all-start = ((bf16[16,2,128,4,256]{4,3,2,1,0:T(4,128)(2,1)}), bf16[16,2,128,4,256]{4,3,2,1,0:T(4,128)(2,1)}, u32[]{:S(2)}, u32[]{:S(2)}) async-start(bf16[16,2,128,4,256]{4,3,2,1,0:T(4,128)(2,1)} %reshape.201), calls=%async_computation | async-start | bytes 16777216 | tf_op jit(solution)/shard_map/all_to_all | solution.py:118
  64.1 2.7 fusion.96
  66.8 2.3 copy.165
  70.5 356.3 %all-gather.1 = f32[16,1,32]{2,1,0:T(1,128)S(1)} all-gather(f32[1,1,32]{2,1,0:T(1,128)S(1)} %bitcast.169), channel_id=1, replica_groups=mesh['ctx'=16,'head'=2] {'ctx'}, dimensions={0}, use_global_device_ids=true | all-gather | bytes 2176 | tf_op jit(solution)/shard_map/all_gather | solution.py:15
  427.0 2.2 pad_add_fusion
  429.2 2.2 pad_add_fusion.1
  431.3 6.9 %fusion.21 = f32[32,256,128]{1,2,0:T(8,128)} fusion(f32[32,256]{1,0:T(8,128)S(1)} %get-tuple-element.138, pred[256,256]{1,0:T(8,128)(4,1)S(1)} %iota_compare_fusion, bf16[256,32,128]{0,2,1:T(8,128)(2,1)} %bitcast.157, bf16[256,4096]{1,0:T(8,128)(2,1)S(1)} %copy-done, bf16[256,4096]{1,0:T(8,128)(2,1)} %param.15), kind=kOutput, calls=%fused_computation.33 | convolution fusion | flops 1090519040 | bytes 10584064 | tf_op jit(solution)/shard_map/hts,shd->thd/dot_general | solution.py:58
  438.3 9.0 %gather_fusion = bf16[16,128,4,256]{3,2,1,0:T(4,128)(2,1)} fusion(bf16[16,2,128,4,256]{4,3,2,1,0:T(4,128)(2,1)} %all-to-all-done, s32[16]{0:T(128)S(1)} %get-tuple-element.147), kind=kCustom, calls=%fused_computation | custom fusion | bytes 8388736 | tf_op jit(solution)/shard_map/gather | solution.py:119
  447.3 4.9 copy.134
  452.2 9.0 %gather_fusion.1 = bf16[16,128,4,256]{3,2,1,0:T(4,128)(2,1)} fusion(bf16[16,2,128,4,256]{4,3,2,1,0:T(4,128)(2,1)} %all-to-all-done, s32[16]{0:T(128)S(1)} %get-tuple-element.148), kind=kCustom, calls=%fused_computation.1 | custom fusion | bytes 8388736 | tf_op jit(solution)/shard_map/gather | solution.py:119
  461.1 5.1 copy.143
  467.5 15.0 %fusion.5 = (f32[4,8,128]{2,1,0:T(8,128)S(1)}, f32[4,2304,128,8]{2,1,3,0:T(8,128)}) fusion(pred[128,2304]{0,1:T(8,128)(4,1)S(1)} %pad_add_fusion, bf16[128,4,8,128]{0,3,2,1:T(8,128)(2,1)S(1)} %bitcast.161, bf16[256,4,128]{2,0,1:T(8,128)(2,1)S(1)} %copy-done.9, bf16[2048,4,128]{2,0,1:T(8,128)(2,1)S(1)} %get-tuple-element.130), kind=kOutput, calls=%fused_computation.14 | convolution fusion | flops 2448945152 | bytes 41467904 | tf_op jit(solution)/shard_map/tkgd,skd->kgts/dot_general | solution.py:132
  482.5 16.0 %fusion.1 = f32[4,8,128]{2,1,0:T(8,128)S(1)} fusion(f32[4,2304,128,8]{2,1,3,0:T(8,128)} %get-tuple-element.146, f32[4,8,128]{2,1,0:T(8,128)S(1)} %get-tuple-element.145, pred[128,2304]{0,1:T(8,128)(4,1)S(1)} %pad_add_fusion), kind=kLoop, calls=%fused_computation.10 | loop fusion | flops 37744640 | bytes 38076416 | tf_op jit(solution)/shard_map/reduce_sum | solution.py:144
  498.6 17.0 %fusion.53 = bf16[128,4,8,128]{0,3,2,1:T(8,128)(2,1)} fusion(f32[4,2304,128,8]{2,1,3,0:T(8,128)} %get-tuple-element.146, f32[4,8,128]{2,1,0:T(8,128)S(1)} %get-tuple-element.145, pred[128,2304]{0,1:T(8,128)(4,1)S(1)} %pad_add_fusion, bf16[256,4,128]{2,0,1:T(8,128)(2,1)S(1)} %copy-done.8, bf16[2048,4,128]{2,0,1:T(8,128)(2,1)S(1)} %get-tuple-element.129, ...), kind=kOutput, calls=%fused_computation.70 | convolution fusion | flops 2459435008 | bytes 41484288 | tf_op jit(solution)/shard_map/kgts,skd->tkgd/dot_general | solution.py:145
  517.1 2.6 fusion.95
  519.7 14.2 %fusion.6 = (f32[4,8,128]{2,1,0:T(8,128)S(1)}, f32[4,2304,128,8]{2,1,3,0:T(8,128)}) fusion(pred[128,2304]{0,1:T(8,128)(4,1)S(1)} %pad_add_fusion.1, bf16[128,4,8,128]{0,3,2,1:T(8,128)(2,1)S(1)} %bitcast.160, bf16[256,4,128]{2,0,1:T(8,128)(2,1)S(1)} %copy-done.10, bf16[2048,4,128]{2,0,1:T(8,128)(2,1)S(1)} %get-tuple-element.132), kind=kOutput, calls=%fused_computation.15 | convolution fusion | flops 2448945152 | bytes 41467904 | tf_op jit(solution)/shard_map/tkgd,skd->kgts/dot_general | solution.py:132
  534.0 16.0 %fusion.3 = f32[4,8,128]{2,1,0:T(8,128)S(1)} fusion(f32[4,2304,128,8]{2,1,3,0:T(8,128)} %get-tuple-element.144, f32[4,8,128]{2,1,0:T(8,128)S(1)} %get-tuple-element.143, pred[128,2304]{0,1:T(8,128)(4,1)S(1)} %pad_add_fusion.1), kind=kLoop, calls=%fused_computation.12 | loop fusion | flops 37744640 | bytes 38076416 | tf_op jit(solution)/shard_map/reduce_sum | solution.py:144
  550.0 17.3 %fusion.52 = bf16[128,4,8,128]{0,3,2,1:T(8,128)(2,1)} fusion(f32[4,2304,128,8]{2,1,3,0:T(8,128)} %get-tuple-element.144, f32[4,8,128]{2,1,0:T(8,128)S(1)} %get-tuple-element.143, pred[128,2304]{0,1:T(8,128)(4,1)S(1)} %pad_add_fusion.1, bf16[256,4,128]{2,0,1:T(8,128)(2,1)} %copy.136, bf16[2048,4,128]{2,0,1:T(8,128)(2,1)S(1)} %get-tuple-element.131, ...), kind=kOutput, calls=%fused_computation.68 | convolution fusion | flops 2459435008 | bytes 41484288 | tf_op jit(solution)/shard_map/kgts,skd->tkgd/dot_general | solution.py:145
  567.3 2.4 copy.151
  569.7 2.7 pad_maximum_fusion.5
  572.4 34.2 %while.14 = (s32[]{:T(128)}, f32[32,128,128]{2,1,0:T(8,128)S(1)}, s32[]{:T(128)}, f32[16,32]{1,0:T(8,128)S(1)}, f32[16,32,128,128]{3,2,1,0:T(8,128)}, /*index=5*/s32[]{:T(128)}, s32[]{:T(128)}) while((s32[]{:T(128)}, f32[32,128,128]{2,1,0:T(8,128)S(1)}, s32[]{:T(128)}, f32[16,32]{1,0:T(8,128)S(1)}, f32[16,32,128,128]{3,2,1,0:T(8,128)}, ...), condition=%wide.region_3.4_spmd.clone, body=%wide.region_2.3_spmd.clone.sunk | while | flops 2097156 | bytes 6291953 | solution.py:27
  572.4 2.1 fusion.113
  574.6 2.1 fusion.113
  576.7 2.1 fusion.113
  578.9 2.1 fusion.113
  581.0 2.1 fusion.113
  583.2 2.1 fusion.113
  585.3 2.1 fusion.113
  587.4 2.1 fusion.113
  589.6 2.1 fusion.113
  591.7 2.1 fusion.113
  593.9 2.1 fusion.113
  596.0 2.1 fusion.113
  598.1 2.1 fusion.113
  600.3 2.1 fusion.113
  602.4 2.1 fusion.113
  606.7 8.0 %multiply_reduce_fusion = (f32[256]{0:T(256)S(1)}, f32[256,32,128]{0,2,1:T(8,128)}) fusion(f32[32,128,128]{2,1,0:T(8,128)S(1)} %get-tuple-element.96, f32[256,32]{0,1:T(8,128)S(1)} %get-tuple-element.135, f32[32,256,128]{1,2,0:T(8,128)} %fusion.21, bf16[256,4096]{1,0:T(8,128)(2,1)} %param.15), kind=kOutput, calls=%fused_computation.37 | convolution fusion | flops 1621098240 | bytes 12616704 | tf_op jit(solution)/shard_map/thd,hde->the/dot_general | solution.py:71
  614.7 12.5 %psum.7 = f32[256]{0:T(256)S(1)} all-reduce(f32[256]{0:T(256)S(1)} %get-tuple-element.141), channel_id=1, replica_groups=mesh['ctx'=16,'head'=2] {'head'}, use_global_device_ids=true, to_apply=%region_5.6 | all-reduce | flops 256 | bytes 2048 | tf_op jit(solution)/shard_map/psum | solution.py:76
  627.2 5.8 copy.133
  633.0 5.4 multiply_convert_fusion.2
  (82 shorter events, 14.2 us)
Async XLA Ops:
  7.2 10.3 %copy-start = (bf16[256,4096]{1,0:T(8,128)(2,1)S(1)}, bf16[256,4096]{1,0:T(8,128)(2,1)}, u32[]{:S(2)}) copy-start(bf16[256,4096]{1,0:T(8,128)(2,1)} %param.17) | copy-start | bytes 6291460
  7.2 565.3 %all-gather.4.cloned.1.call-start = ((), (), s32[]{:S(2)}) async-start(), calls=%async_computation.1 | async-start | bytes 35651584 | tf_op jit(solution)/shard_map/all_gather | solution.py:15
  26.4 8.3 %copy-start.11 = (s32[32,16]{0,1:T(8,128)S(1)}, s32[32,16]{0,1:T(8,128)}, u32[]{:S(2)}) copy-start(s32[32,16]{0,1:T(8,128)} %param.26) | copy-start | bytes 6148
  53.3 6.7 %copy-start.13 = (s32[32]{0:T(128)S(1)}, s32[32]{0:T(128)}, u32[]{:S(2)}) copy-start(s32[32]{0:T(128)} %param.27) | copy-start | bytes 388
  53.3 8.8 %copy-start.6 = (bf16[256,512]{1,0:T(8,128)(2,1)S(1)}, bf16[256,512]{1,0:T(8,128)(2,1)}, u32[]{:S(2)}) copy-start(bf16[256,512]{1,0:T(8,128)(2,1)} %param.22) | copy-start | bytes 786436
  53.3 9.8 %copy-start.7 = (bf16[256,512]{1,0:T(8,128)(2,1)S(1)}, bf16[256,512]{1,0:T(8,128)(2,1)}, u32[]{:S(2)}) copy-start(bf16[256,512]{1,0:T(8,128)(2,1)} %param.23) | copy-start | bytes 786436
  53.3 385.0 %all-to-all-start = ((bf16[16,2,128,4,256]{4,3,2,1,0:T(4,128)(2,1)}), bf16[16,2,128,4,256]{4,3,2,1,0:T(4,128)(2,1)}, u32[]{:S(2)}, u32[]{:S(2)}) async-start(bf16[16,2,128,4,256]{4,3,2,1,0:T(4,128)(2,1)} %reshape.201), calls=%async_computation | async-start | bytes 16777216 | tf_op jit(solution)/shard_map/all_to_all | solution.py:118
  461.1 5.1 copy-start.3
  466.2 1.2 copy-start.5
  466.2 1.3 copy-start.9
  482.5 16.0 %copy-start.8 = (bf16[256,4,128]{2,0,1:T(8,128)(2,1)S(1)}, bf16[256,4,128]{2,0,1:T(8,128)(2,1)}, u32[]{:S(2)}) copy-start(bf16[256,4,128]{2,0,1:T(8,128)(2,1)} %copy.136) | copy-start | bytes 786436
  517.1 2.6 copy-start.4
  517.1 2.6 copy-start.10
  567.3 5.2 copy-start.2
  627.2 5.8 copy-start.12
  627.2 11.1 %copy-start.1 = (bf16[256,4096]{1,0:T(8,128)(2,1)S(1)}, bf16[256,4096]{1,0:T(8,128)(2,1)}, u32[]{:S(2)}) copy-start(bf16[256,4096]{1,0:T(8,128)(2,1)} %param.17) | copy-start | bytes 6291460
Sparse Core Ops, SparseCore 0:
  23.0 515.3 all-gather.3
where the time goes:
time: 656 us; the launch traced here: 646 us
  blocking collectives  369 us (56%)
  matrix products  91.3 us (14%)
  other arithmetic  88.3 us (13%)
  local copies, waits for them, and re-layouts  75.2 us (11%)
  between operations  14.7 us (2%)
  starting transfers between devices  6.7 us (1%)
    all_gather x1, blocking collectives, entering_2(): everything = jax.tree.map(lambda part: lax.all_gather(part, axis), array)  356 us
    dot_general x2, matrix products, cache_attention(): jnp.einsum('kgts,skd->tkgd', weights.astype(jnp.bfloat16), all_values, pr...  34.3 us
    select_n x16, other arithmetic, turn(): return jax.tree.map(lambda a, b: jnp.where(reached, a, b), new, before)  33.6 us
    reduce_sum x2, other arithmetic, cache_attention(): totals = jnp.sum(weights, axis=3)  32 us
    dot_general x2, matrix products, cache_attention(): jnp.einsum('tkgd,skd->kgts', queries, all_keys, preferred_element_type=jn...  29.3 us
    gather x4, local copies, waits for them, and re-layouts, cache_attention(): arrived[my_owners[block_index], block_index]  28 us
  transfers between devices with their start and end apart: 2, of which 0 were waited for; matrix products, arithmetic and copies ran while one was open for 29% of the time, Pallas kernels for 0%

commit v1 on v0

v1 whole, which is shorter than its diff:
```python
import functools
import math

import jax
import jax.numpy as jnp
from jax import lax
from jax.experimental import pallas as pl
from jax.experimental.pallas import tpu as pltpu
from jax.sharding import PartitionSpec as P

HD = 128
BLOCK = 128
STEP_HEADS = 8
PAD = 16
VMEM_LIMIT = 56 * 1024 * 1024
F32 = jnp.float32
BF16 = jnp.bfloat16
NT = (((1,), (1,)), ((), ()))
TN = (((0,), (0,)), ((), ()))


def params(**more):
    return pltpu.CompilerParams(vmem_limit_bytes=VMEM_LIMIT, **more)


def cost(microseconds):
    return pl.CostEstimate(
        flops=0, bytes_accessed=int(microseconds * 3.69e6), transcendentals=0
    )


def silu(u):
    half = u.astype(F32) * 0.5
    return (half + half * jnp.tanh(half)).astype(BF16)


def pack_kernel(first, spots, keys, values, *rest):
    outs, sems = rest[:-1], rest[-1]
    copies = []
    start = first
    for part, out in enumerate(outs):
        width = out.shape[3]
        for dest in range(out.shape[0]):
            rows = pl.ds(pl.multiple_of(spots[dest] * BLOCK, BLOCK), BLOCK)
            for kind, source in enumerate((keys, values)):
                copies.append(
                    pltpu.make_async_copy(
                        source.at[rows, pl.ds(start, width)],
                        out.at[dest, kind],
                        sems.at[part, dest, kind],
                    )
                )
        start += width
    for copy in copies:
        copy.start()
    for copy in copies:
        copy.wait()


def pack(spots, keys, values, first, widths):
    n = spots.shape[0]
    whole = pl.BlockSpec(keys.shape, lambda i, _: (0, 0))
    return pl.pallas_call(
        functools.partial(pack_kernel, first),
        out_shape=[jax.ShapeDtypeStruct((n, 2, BLOCK, width), BF16) for width in widths],
        grid_spec=pltpu.PrefetchScalarGridSpec(
            num_scalar_prefetch=1,
            grid=(1,),
            in_specs=[whole, whole],
            out_specs=[pl.BlockSpec(memory_space=pl.ANY)] * len(widths),
            scratch_shapes=[pltpu.SemaphoreType.DMA((len(widths), n, 2))],
        ),
        compiler_params=params(),
        cost_estimate=cost(4),
        name="pack",
    )(spots, keys, values)


def state_kernel(group, place, keys, values, decay, running_out, *rest):
    outs, running, hold = rest[:group], rest[group], rest[group + 1]
    step = pl.program_id(0)
    rows = keys.shape[0]
    mine = place[0]
    per = hold.shape[1] // HD

    @pl.when(step == 0)
    def _():
        s = lax.broadcasted_iota(jnp.int32, (rows, rows), 0)
        t = lax.broadcasted_iota(jnp.int32, (rows, rows), 1)
        running[...] = lax.dot_general(
            decay[...],
            (s <= t).astype(F32),
            TN,
            precision=lax.Precision.HIGHEST,
            preferred_element_type=F32,
        )

    here = running[pl.ds(pl.multiple_of(step * STEP_HEADS, STEP_HEADS), STEP_HEADS), :]
    running_out[...] = here
    total = here[:, rows - 1 : rows]
    fade = jnp.exp(total - here)
    wide = jnp.broadcast_to(total, (STEP_HEADS, HD))
    high = wide.astype(BF16).astype(F32)
    middle = (wide - high).astype(BF16).astype(F32)
    low = wide - high - middle
    for dest in range(STEP_HEADS // per):
        slot = (step * (STEP_HEADS // per) + dest) ^ mine
        for i in range(per):
            head = dest * per + i
            columns = slice(head * HD, (head + 1) * HD)
            act = silu(keys[:, columns]).T
            state = jnp.dot(
                (act.astype(F32) * fade[head : head + 1, :]).astype(BF16),
                values[:, columns],
                preferred_element_type=F32,
            )
            hold[slot, i * HD : (i + 1) * HD, :] = state.astype(BF16)
        mine_rows = slice(dest * per, (dest + 1) * per)
        tail = [high[mine_rows], middle[mine_rows], low[mine_rows]]
        if 3 * per < PAD:
            tail.append(jnp.zeros((PAD - 3 * per, HD), F32))
        hold[slot, per * HD :, :] = jnp.concatenate(tail, axis=0).astype(BF16)

    @pl.when(step == pl.num_programs(0) - 1)
    def _():
        for k, out in enumerate(outs):
            out[...] = hold[k]


def segment_states(keys, values, decay, place, group):
    rows, heads = decay.shape
    per = heads // group
    size = per * HD + PAD
    wide = STEP_HEADS * HD
    return pl.pallas_call(
        functools.partial(state_kernel, group),
        out_shape=[jax.ShapeDtypeStruct((heads, rows), F32)]
        + [jax.ShapeDtypeStruct((size, HD), BF16)] * group,
        grid_spec=pltpu.PrefetchScalarGridSpec(
            num_scalar_prefetch=1,
            grid=(heads // STEP_HEADS,),
            in_specs=[
                pl.BlockSpec((rows, wide), lambda i, _: (0, i)),
                pl.BlockSpec((rows, wide), lambda i, _: (0, i)),
                pl.BlockSpec((rows, heads), lambda i, _: (0, 0)),
            ],
            out_specs=[pl.BlockSpec((STEP_HEADS, rows), lambda i, _: (i, 0))]
            + [pl.BlockSpec((size, HD), lambda i, _: (0, 0))] * group,
            scratch_shapes=[pltpu.VMEM((heads, rows), F32), pltpu.VMEM((group, size, HD), BF16)],
        ),
        compiler_params=params(),
        cost_estimate=cost(6),
        name="segment_states",
    )(place, keys, values, decay)


def intra_kernel(queries, keys, values, running, out):
    rows = queries.shape[0]
    column = running[...].T
    t = lax.broadcasted_iota(jnp.int32, (BLOCK, BLOCK), 0)
    s = lax.broadcasted_iota(jnp.int32, (BLOCK, BLOCK), 1)
    causal = s <= t
    for head in range(STEP_HEADS):
        columns = slice(head * HD, (head + 1) * HD)
        act_q = silu(queries[:, columns])
        act_k = silu(keys[:, columns])
        v = values[:, columns]
        for a in range(rows // BLOCK):
            mine = slice(a * BLOCK, (a + 1) * BLOCK)
            seen = (a + 1) * BLOCK
            scores = lax.dot_general(act_q[mine], act_k[:seen], NT, preferred_element_type=F32)
            gaps = column[mine, head : head + 1] - running[head : head + 1, :seen]
            pieces = []
            for b in range(a + 1):
                part = slice(b * BLOCK, (b + 1) * BLOCK)
                gap = jnp.minimum(gaps[:, part], 0.0)
                if b == a:
                    gap = jnp.where(causal, gap, -1e30)
                pieces.append((scores[:, part] * jnp.exp(gap)).astype(BF16))
            weights = pieces[0] if a == 0 else jnp.concatenate(pieces, axis=1)
            out[mine, columns] = jnp.dot(weights, v[:seen], preferred_element_type=F32)


def intra(queries, keys, values, running):
    rows, features = queries.shape
    wide = STEP_HEADS * HD
    block = pl.BlockSpec((rows, wide), lambda i: (0, i))
    return pl.pallas_call(
        intra_kernel,
        out_shape=jax.ShapeDtypeStruct((rows, features), F32),
        grid=(features // wide,),
        in_specs=[block, block, block, pl.BlockSpec((STEP_HEADS, rows), lambda i: (i, 0))],
        out_specs=block,
        compiler_params=params(),
        cost_estimate=cost(10),
        name="intra",
    )(queries, keys, values, running)


def read_total(message, per, head):
    base = per * HD + head
    rows = [message[base + k * per : base + k * per + 1, :].astype(F32) for k in range(3)]
    return rows[0] + rows[1] + rows[2]


def walk_kernel(group, per, with_start, place, *refs):
    arrived = refs[:group]
    mine = place[0]
    if with_start:
        start, outs, hold = refs[group], refs[group + 1 : -1], refs[-1]
    else:
        outs, hold = refs[group:-1], refs[-1]
    for k in range(group):
        hold[mine ^ k] = arrived[k][...]
    for head in range(per):
        rows = slice(head * HD, (head + 1) * HD)
        if with_start:
            state = start[rows, :].astype(F32)
        else:
            state = jnp.zeros((HD, HD), F32)
        for j in range(group):
            message = hold.at[j]
            own = message[rows, :].astype(F32)
            fade = jnp.exp(read_total(message[...], per, head))
            if with_start:
                hold[j, rows, :] = state.astype(BF16)
            state = fade * state + own
        if not with_start:
            outs[0][rows, :] = state.astype(outs[0].dtype)
    if with_start:
        for k in range(group):
            outs[k][...] = hold[mine ^ k, : per * HD, :]


def walk(arrived, place, start=None):
    group = len(arrived)
    size = arrived[0].shape[0]
    per = (size - PAD) // HD
    whole = pl.BlockSpec((size, HD), lambda i, _: (0, 0))
    part = pl.BlockSpec((per * HD, HD), lambda i, _: (0, 0))
    with_start = start is not None
    outs = group if with_start else 1
    return pl.pallas_call(
        functools.partial(walk_kernel, group, per, with_start),
        out_shape=[jax.ShapeDtypeStruct((per * HD, HD), BF16)] * outs,
        grid_spec=pltpu.PrefetchScalarGridSpec(
            num_scalar_prefetch=1,
            grid=(1,),
            in_specs=[whole] * group + [part] * with_start,
            out_specs=[part] * outs,
            scratch_shapes=[pltpu.VMEM((group, size, HD), BF16)],
        ),
        compiler_params=params(),
        cost_estimate=cost(2.5),
        name="walk_states",
    )(place, *arrived, *((start,) if with_start else ()))


def join_kernel(group, place, queries, inside, running, *refs):
    states, (out, squares), (hold, total) = refs[:group], refs[group : group + 2], refs[group + 2 :]
    step = pl.program_id(0)
    mine = place[0]
    per = hold.shape[1] // HD

    @pl.when(step == 0)
    def _():
        for k in range(group):
            hold[mine ^ k] = states[k][...]
        total[...] = jnp.zeros_like(total)

    grow = jnp.exp(running[...].T)
    summed = jnp.zeros(total.shape, F32)
    for head in range(STEP_HEADS):
        columns = slice(head * HD, (head + 1) * HD)
        owner = step * (STEP_HEADS // per) + head // per
        part = (head % per) * HD
        passed = jnp.dot(
            silu(queries[:, columns]), hold[owner, part : part + HD, :], preferred_element_type=F32
        )
        attn = inside[:, columns] + grow[:, head : head + 1] * passed
        out[:, columns] = attn
        summed += attn * attn
    total[...] += summed

    @pl.when(step == pl.num_programs(0) - 1)
    def _():
        squares[...] = lax.dot_general(
            jnp.ones((8, HD), F32),
            total[...],
            NT,
            precision=lax.Precision.HIGHEST,
            preferred_element_type=F32,
        )


def join(queries, inside, running, states, place):
    rows, features = queries.shape
    wide = STEP_HEADS * HD
    block = pl.BlockSpec((rows, wide), lambda i, _: (0, i))
    group = len(states)
    return pl.pallas_call(
        functools.partial(join_kernel, group),
        out_shape=[
            jax.ShapeDtypeStruct((rows, features), F32),
            jax.ShapeDtypeStruct((8, rows), F32),
        ],
        grid_spec=pltpu.PrefetchScalarGridSpec(
            num_scalar_prefetch=1,
            grid=(features // wide,),
            in_specs=[block, block, pl.BlockSpec((STEP_HEADS, rows), lambda i, _: (i, 0))]
            + [pl.BlockSpec(state.shape, lambda i, _: (0, 0)) for state in states],
            out_specs=[block, pl.BlockSpec((8, rows), lambda i, _: (0, 0))],
            scratch_shapes=[
                pltpu.VMEM((group,) + states[0].shape, BF16),
                pltpu.VMEM((rows, HD), F32),
            ],
        ),
        compiler_params=params(),
        cost_estimate=cost(7),
        name="join_states",
    )(place, queries, inside, running, *states)


def gate_kernel(features, attn, gate, gain, *refs):
    out = refs[-1]
    squares = refs[0][...]
    for more in refs[1:-1]:
        squares = squares + more[...]
    scaling = lax.rsqrt(squares / features + 1e-06).T[:, :1]
    half = gate[...].astype(F32) * 0.5
    opened = 0.5 + 0.5 * jnp.tanh(half)
    out[...] = (attn[...] * scaling * gain[...] * opened).astype(BF16)


def gated(attn, gate, gain, squares, features):
    rows, here = attn.shape
    wide = STEP_HEADS * HD
    block = pl.BlockSpec((rows, wide), lambda i: (0, i))
    return pl.pallas_call(
        functools.partial(gate_kernel, features),
        out_shape=jax.ShapeDtypeStruct((rows, here), BF16),
        grid=(here // wide,),
        in_specs=[block, block, pl.BlockSpec((1, wide), lambda i: (0, i))]
        + [pl.BlockSpec((8, rows), lambda i: (0, 0))] * len(squares),
        out_specs=block,
        compiler_params=params(),
        cost_estimate=cost(6),
        name="gated_norm",
    )(attn, gate, gain.reshape(1, here), *squares)


def exchange_in_group(messages, group):
    n = lax.axis_size("ctx")
    return [messages[0]] + [
        lax.ppermute(messages[k], "ctx", [(i, i ^ k) for i in range(n)]) for k in range(1, group)
    ]


def states_before_group(total, logs, group):
    n = lax.axis_size("ctx")
    groups = n // group

    def shift(array, by):
        return lax.ppermute(
            array, "ctx", [(i, i + by * group) for i in range(n - by * group)]
        )

    before = shift(total, 1)
    if groups == 2:
        return before
    span = shift(logs, 1)
    reach = 1
    while reach < groups - 1:
        far = shift(before, reach).astype(F32)
        before = (
            far * jnp.exp(span)[:, None] + before.astype(F32)
        ).astype(BF16)
        span = span + shift(span, reach)
        reach *= 2
    return before


def soft_kernel(
    chosen, owners, counts, queries, slab_k, slab_v, arrived, *refs
):
    out, scores, top, weight_sum, mixed = refs[-5:]
    b = pl.program_id(1)
    count = counts[b]
    heads = queries.shape[1] // HD
    chunk = 2 * BLOCK
    chunks = heads * BLOCK // chunk
    scale = math.log2(math.e) / math.sqrt(HD)
    low = -1e30

    def rows_of(r):
        return jnp.concatenate(
            [queries[:, (2 * r + i) * HD : (2 * r + i + 1) * HD] for i in range(2)], axis=0
        )

    def pair(kind, first, second):
        return jnp.concatenate(
            [
                arrived[owners[b * chosen + first], kind],
                arrived[owners[b * chosen + second], kind],
            ],
            axis=0,
        )

    def score(tile, k, allowed, first):
        for r in range(chunks):
            at = slice(r * chunk, (r + 1) * chunk)
            s = lax.dot_general(rows_of(r), k, NT, preferred_element_type=F32)
            if allowed is not None:
                s = jnp.where(allowed, s, low)
            scores[tile, at, :] = s
            here = jnp.maximum(s[:, :BLOCK], s[:, BLOCK:])
            top[at, :] = here if first else jnp.maximum(top[at, :], here)

    t = lax.broadcasted_iota(jnp.int32, (chunk, chunk), 0) % BLOCK
    s_at = lax.broadcasted_iota(jnp.int32, (chunk, chunk), 1)
    score(0, slab_k[...], s_at <= t + b * BLOCK, True)
    pairs = count // 2

    def score_pair(p, _):
        score(p + 1, pair(0, 2 * p, 2 * p + 1), None, False)
        return 0

    lax.fori_loop(0, pairs, score_pair, 0)
    odd = count % 2 == 1

    @pl.when(odd)
    def _():
        score(pairs + 1, pair(0, count - 1, count - 1), s_at < BLOCK, False)

    for r in range(chunks):
        at = slice(r * chunk, (r + 1) * chunk)
        highest = jnp.max(top[at, :], axis=1, keepdims=True) * scale
        top[at, :] = jnp.broadcast_to(highest, (chunk, BLOCK))

    def mix(tile, v, first):
        for r in range(chunks):
            at = slice(r * chunk, (r + 1) * chunk)
            highest = top[at, :]
            left = jnp.exp2(scores[tile, at, :BLOCK] * scale - highest)
            right = jnp.exp2(scores[tile, at, BLOCK:] * scale - highest)
            w = jnp.concatenate([left.astype(BF16), right.astype(BF16)], axis=1)
            more = jnp.dot(w, v, preferred_element_type=F32)
            if first:
                weight_sum[at, :] = left + right
                mixed[at, :] = more
            else:
                weight_sum[at, :] += left + right
                mixed[at, :] += more

    mix(0, slab_v[...], True)

    def mix_pair(p, _):
        mix(p + 1, pair(1, 2 * p, 2 * p + 1), False)
        return 0

    lax.fori_loop(0, pairs, mix_pair, 0)

    @pl.when(odd)
    def _():
        mix(pairs + 1, pair(1, count - 1, count - 1), False)

    for head in range(heads):
        at = slice(head * BLOCK, (head + 1) * BLOCK)
        total = jnp.sum(weight_sum[at, :], axis=1, keepdims=True)
        out[:, head * HD : (head + 1) * HD] = (mixed[at, :] / total).astype(BF16)


def soft_part(owners, counts, queries, slab_k, slab_v, arrived, first, chosen, so_far):
    rows, features = queries.shape
    kv_here = arrived.shape[3] // HD
    n = arrived.shape[0]
    wide = features // (slab_k.shape[1] // HD)
    blocks = rows // BLOCK
    grid_spec = pltpu.PrefetchScalarGridSpec(
        num_scalar_prefetch=2,
        grid=(kv_here, blocks),
        in_specs=[
            pl.BlockSpec((BLOCK, wide), lambda h, b, *_: (b, first + h)),
            pl.BlockSpec((rows, HD), lambda h, b, *_: (0, first + h)),
            pl.BlockSpec((rows, HD), lambda h, b, *_: (0, first + h)),
            pl.BlockSpec((n, 2, BLOCK, HD), lambda h, b, *_: (0, 0, 0, h)),
        ]
        + ([] if so_far is None else [pl.BlockSpec(memory_space=pl.ANY)]),
        out_specs=pl.BlockSpec((BLOCK, wide), lambda h, b, *_: (b, first + h)),
        scratch_shapes=[
            pltpu.VMEM((chosen // 2 + 2, wide // HD * BLOCK, 2 * BLOCK), F32),
            pltpu.VMEM((wide // HD * BLOCK, BLOCK), F32),
            pltpu.VMEM((wide // HD * BLOCK, BLOCK), F32),
            pltpu.VMEM((wide // HD * BLOCK, BLOCK), F32),
        ],
    )
    return pl.pallas_call(
        functools.partial(soft_kernel, chosen),
        out_shape=jax.ShapeDtypeStruct((rows, features), BF16),
        grid_spec=grid_spec,
        input_output_aliases={} if so_far is None else {6: 0},
        compiler_params=params(),
        cost_estimate=cost(9 * kv_here),
        name="soft_attention",
    )(owners, counts, queries, slab_k, slab_v, arrived, *(() if so_far is None else (so_far,)))


def parts_of(kv_count):
    return [kv_count] if kv_count < 2 else [kv_count - 1, 1]


def local(
    lin_queries,
    lin_keys,
    lin_values,
    log_decay,
    lin_gate,
    norm_gain,
    soft_queries,
    slab_keys,
    slab_values,
    cache_keys,
    cache_values,
    block_lists,
    live_counts,
):
    n = lax.axis_size("ctx")
    me = lax.axis_index("ctx")
    head_devices = lax.axis_size("head")
    heads = log_decay.shape[1]
    chosen = block_lists.shape[1]
    kv_count = cache_keys.shape[1] // HD
    stored = cache_keys.shape[0] // BLOCK
    blocks_here = block_lists.shape[0] // n
    group = 1
    while group < 8 and 2 * group <= n and heads % (2 * group) == 0:
        group *= 2
    per = heads // group

    lists = block_lists.reshape(n, blocks_here, chosen)
    counts = live_counts.reshape(n, blocks_here)
    live = jnp.arange(chosen)[None, None, :] < counts[:, :, None]
    owner = lists // stored
    spots = jnp.max(jnp.where(live & (owner == me), lists % stored, 0), axis=(1, 2))
    my_owners = lax.dynamic_slice_in_dim(owner, me, 1, 0).reshape(blocks_here * chosen)
    my_counts = lax.dynamic_slice_in_dim(counts, me, 1, 0).reshape(blocks_here)
    place = (me % group).reshape(1)

    parts = parts_of(kv_count)
    outgoing = pack(spots, cache_keys, cache_values, 0, [part * HD for part in parts])

    running, *messages = segment_states(lin_keys, lin_values, log_decay, place, group)
    messages = exchange_in_group(messages, group)
    (total,) = walk(messages, place)
    logs = None
    if n // group > 2:
        logs = sum(
            message[per * HD : per * HD + 3 * per, 0].astype(F32).reshape(3, per).sum(0)
            for message in messages
        )
        logs = jnp.repeat(logs, HD)
    before = states_before_group(total, logs, group)
    states = exchange_in_group(walk(messages, place, before), group)

    inside = intra(lin_queries, lin_keys, lin_values, running)
    attn, squares = join(lin_queries, inside, running, states, place)
    arrived = [lax.all_to_all(outgoing[0], "ctx", 0, 0, tiled=True)]
    for block in outgoing[1:]:
        block, attn = lax.optimization_barrier((block, attn))
        arrived.append(lax.all_to_all(block, "ctx", 0, 0, tiled=True))
    summands = [squares]
    reach = 1
    while reach < head_devices:
        if len(summands) > 1:
            summands = [summands[0] + summands[1]]
        summands.append(
            lax.ppermute(summands[0], "head", [(i, i ^ reach) for i in range(head_devices)])
        )
        reach *= 2
    features = head_devices * heads * HD
    lin_out = gated(attn, lin_gate, norm_gain, summands, features)

    soft_out = None
    first = 0
    for part, block in zip(parts, arrived):
        soft_out = soft_part(
            my_owners, my_counts, soft_queries, slab_keys, slab_values, block, first, chosen, soft_out
        )
        first += part
    return (lin_out, soft_out)


def solution(mesh):
    in_specs = (
        P("ctx", "head"),
        P("ctx", "head"),
        P("ctx", "head"),
        P("ctx", "head"),
        P("ctx", "head"),
        P("head"),
        P("ctx", "head"),
        P("ctx", "head"),
        P("ctx", "head"),
        P("ctx", "head"),
        P("ctx", "head"),
        P(),
        P(),
    )
    out_specs = (P("ctx", "head"), P("ctx", "head"))
    return jax.shard_map(local, mesh=mesh, in_specs=in_specs, out_specs=out_specs, check_vma=False)
```

time: 656 us -> 195 us (0.30)
  the two profiles are of different devices: /device:TPU:17 before, /device:TPU:25 now
where the time goes in v1:
time: 195 us; the launch traced here: 194 us
  Pallas kernels  90.9 us (47%)
  waiting for transfers between devices  61.7 us (32%)
  starting transfers between devices  34.7 us (18%)
  local copies, waits for them, and re-layouts  4.76 us (2%)
    pallas_call x2, Pallas kernels, soft_part(): pl.pallas_call(functools.partial(soft_kernel, chosen), out_shape=jax.Shap...  53.2 us
    ppermute x14, waiting for transfers between devices, exchange_in_group(): lax.ppermute(messages[k], 'ctx', [(i, i ^ k) for i in range(n)])  51.5 us
    ppermute x14, starting transfers between devices, exchange_in_group(): lax.ppermute(messages[k], 'ctx', [(i, i ^ k) for i in range(n)])  12.3 us
    ppermute x1, waiting for transfers between devices, shift(): lax.ppermute(array, 'ctx', [(i, i + by * group) for i in range(n - by * g...  10.2 us
    pallas_call x1, Pallas kernels, intra(): pl.pallas_call(intra_kernel, out_shape=jax.ShapeDtypeStruct((rows, featur...  9.91 us
    ppermute x1, starting transfers between devices, local(): lax.ppermute(summands[0], 'head', [(i, i ^ reach) for i in range(head_dev...  9.18 us
    pallas_call x1, Pallas kernels, join(): pl.pallas_call(functools.partial(join_kernel, group), out_shape=[jax.Shap...  7.16 us
    all_to_all x1, starting transfers between devices, local(): arrived = [lax.all_to_all(outgoing[0], 'ctx', 0, 0, tiled=True)]  6.45 us
  transfers between devices with their start and end apart: 18, of which 8 were waited for; matrix products, arithmetic and copies ran while one was open for 1% of the time, Pallas kernels for 37%

profile of v1, /device:TPU:25, one launch (start us, length us, event | category | flops | bytes accessed | tf_op | source)
XLA Modules:
  0.0 194.3 jit_solution(15047931714109375920)
XLA Ops:
  0.6 0.7 fusion.2
  1.4 0.1 reduce_max.14
  1.4 0.6 reduce_max.18.spots
  2.1 4.8 %pack.1 = (bf16[16,2,128,384]{3,2,1,0:T(8,128)(2,1)}, bf16[16,2,128,128]{3,2,1,0:T(8,128)(2,1)}) custom-call(s32[16]{0:T(128)} %reduce_max.18.spots, bf16[1024,512]{1,0:T(8,128)(2,1)} %keys.3, bf16[1024,512]{1,0:T(8,128)(2,1)} %values.3), custom_call_target="tpu_custom_call" | custom-call | bytes 14760000 | tf_op jit(solution)/shard_map/pack/pallas_call | solution.py:63
  6.9 6.5 %all-to-all-start.1 = ((bf16[16,2,128,384]{3,2,1,0:T(8,128)(2,1)}), bf16[16,2,128,384]{3,2,1,0:T(8,128)(2,1)S(1)}, u32[]{:S(2)}, u32[]{:S(2)}) async-start(bf16[16,2,128,384]{3,2,1,0:T(8,128)(2,1)} %get-tuple-element.47), calls=%async_computation.1 | async-start | bytes 6291456 | tf_op jit(solution)/shard_map/all_to_all | solution.py:567
  13.3 0.7 copy.21.decay
  14.1 5.5 %segment_states.1 = (f32[32,256]{1,0:T(8,128)}, bf16[528,128]{1,0:T(8,128)(2,1)}, bf16[528,128]{1,0:T(8,128)(2,1)}, bf16[528,128]{1,0:T(8,128)(2,1)}, bf16[528,1...) custom-call(s32[1]{0:T(128)} %bitcast.place, ...), custom_call_target="tpu_custom_call" | custom-call | bytes 22140000 | tf_op jit(solution)/shard_map/segment_states/pallas_call | solution.py:135
  19.6 1.2 collective-permute-start
  20.8 1.2 collective-permute-start.1
  22.0 0.3 collective-permute-start.2
  22.3 0.3 collective-permute-start.3
  22.6 2.1 %collective-permute-start.4 = (bf16[528,128]{1,0:T(8,128)(2,1)}, bf16[528,128]{1,0:T(8,128)(2,1)S(1)}, u32[]{:S(2)}, u32[]{:S(2)}) collective-permute-start(bf16[528,128]{1,0:T(8,128)(2,1)} %get-tuple-element.32), channel_id=1, source_target_pairs={{0,10},{2,8},{4,14},{6,12},{8,2},{10,0},{12,6},{14,4},{16,26},{18,... | collective-permute-start | bytes 405512 | tf_op jit(solution)/shard_map/ppermute | solution.py:355
  24.6 8.4 %collective-permute-done.refs_1_ = bf16[528,128]{1,0:T(8,128)(2,1)S(1)} collective-permute-done((bf16[528,128]{1,0:T(8,128)(2,1)}, bf16[528,128]{1,0:T(8,128)(2,1)S(1)}, u32[]{:S(2)}, u32[]{:S(2)}) %collective-permute-start) | collective-permute-done | bytes 135200 | tf_op jit(solution)/shard_map/ppermute | solution.py:355
  33.0 9.0 %collective-permute-done.1.refs_2_ = bf16[528,128]{1,0:T(8,128)(2,1)S(1)} collective-permute-done((bf16[528,128]{1,0:T(8,128)(2,1)}, bf16[528,128]{1,0:T(8,128)(2,1)S(1)}, u32[]{:S(2)}, u32[]{:S(2)}) %collective-permute-start.1) | collective-permute-done | bytes 135200 | tf_op jit(solution)/shard_map/ppermute | solution.py:355
  42.1 25.2 %collective-permute-done.3.refs_4_ = bf16[528,128]{1,0:T(8,128)(2,1)S(1)} collective-permute-done((bf16[528,128]{1,0:T(8,128)(2,1)}, bf16[528,128]{1,0:T(8,128)(2,1)S(1)}, u32[]{:S(2)}, u32[]{:S(2)}) %collective-permute-start.3) | collective-permute-done | bytes 135200 | tf_op jit(solution)/shard_map/ppermute | solution.py:355
  67.3 2.9 %collective-permute-done.4.refs_5_ = bf16[528,128]{1,0:T(8,128)(2,1)S(1)} collective-permute-done((bf16[528,128]{1,0:T(8,128)(2,1)}, bf16[528,128]{1,0:T(8,128)(2,1)S(1)}, u32[]{:S(2)}, u32[]{:S(2)}) %collective-permute-start.4) | collective-permute-done | bytes 135200 | tf_op jit(solution)/shard_map/ppermute | solution.py:355
  70.2 2.9 %collective-permute-done.5.refs_6_ = bf16[528,128]{1,0:T(8,128)(2,1)S(1)} collective-permute-done((bf16[528,128]{1,0:T(8,128)(2,1)}, bf16[528,128]{1,0:T(8,128)(2,1)S(1)}, u32[]{:S(2)}, u32[]{:S(2)}) %collective-permute-start.5) | collective-permute-done | bytes 135200 | tf_op jit(solution)/shard_map/ppermute | solution.py:355
  73.1 2.9 %collective-permute-done.6.refs_7_ = bf16[528,128]{1,0:T(8,128)(2,1)S(1)} collective-permute-done((bf16[528,128]{1,0:T(8,128)(2,1)}, bf16[528,128]{1,0:T(8,128)(2,1)S(1)}, u32[]{:S(2)}, u32[]{:S(2)}) %collective-permute-start.6) | collective-permute-done | bytes 135200 | tf_op jit(solution)/shard_map/ppermute | solution.py:355
  76.0 0.6 copy-done.7
  76.7 2.2 %walk_states.2 = bf16[512,128]{1,0:T(8,128)(2,1)} custom-call(s32[1]{0:T(128)} %bitcast.place, bf16[528,128]{1,0:T(8,128)(2,1)} %get-tuple-element.27.refs_0_, bf16[528,128]{1,0:T(8,128)(2,1)} %copy-done.1, bf16[528,128]{1,0:T(8,128)(2,1)} %copy-done.2, bf16[528,128]{1,0:T(8,128)(2,1)} %copy-done.3, bf16[528,128]{1,0:T(8,128)(2,1)} %copy-done.4, ...), custom_call_target="tpu_custom_call" | custom-call | bytes 9225000 | tf_op jit(solution)/shard_map/walk_states/pallas_call | solution.py:243
  78.9 1.3 collective-permute-start.7
  80.2 10.2 %collective-permute-done.7.refs_8_ = bf16[512,128]{1,0:T(8,128)(2,1)S(1)} collective-permute-done((bf16[512,128]{1,0:T(8,128)(2,1)}, bf16[512,128]{1,0:T(8,128)(2,1)S(1)}, u32[]{:S(2)}, u32[]{:S(2)}) %collective-permute-start.7) | collective-permute-done | bytes 131104 | tf_op jit(solution)/shard_map/ppermute | solution.py:364
  90.4 0.6 copy-done.8
  91.0 2.7 %walk_states.3 = (bf16[512,128]{1,0:T(8,128)(2,1)}, bf16[512,128]{1,0:T(8,128)(2,1)}, bf16[512,128]{1,0:T(8,128)(2,1)}, bf16[512,128]{1,0:T(8,128)(2,1)}, bf16[5...) custom-call(s32[1]{0:T(128)} %bitcast.place, ...), custom_call_target="tpu_custom_call" | custom-call | bytes 9225000 | tf_op jit(solution)/shard_map/walk_states/pallas_call | solution.py:243
  93.7 0.9 collective-permute-start.11
  94.6 1.6 collective-permute-start.12
  96.1 1.1 collective-permute-start.13
  97.3 1.2 collective-permute-start.14
  98.5 0.1 collective-permute-done.10.refs_3_
  98.6 1.2 collective-permute-start.8
  99.8 1.3 collective-permute-start.9
  101.1 9.9 %intra.1.inside = f32[256,4096]{1,0:T(8,128)} custom-call(bf16[256,4096]{1,0:T(8,128)(2,1)} %queries.5, bf16[256,4096]{1,0:T(8,128)(2,1)} %keys.5, bf16[256,4096]{1,0:T(8,128)(2,1)} %values.5, f32[32,256]{1,0:T(8,128)} %get-tuple-element.26.running), custom_call_target="tpu_custom_call" | custom-call | bytes 36900000 | tf_op jit(solution)/shard_map/intra/pallas_call | solution.py:188
  111.1 0.6 copy-done.11
  111.7 0.0 copy-done.12
  111.7 0.1 copy-done.13
  111.8 0.0 copy-done.14
  111.8 0.0 copy-done.15
  111.9 7.2 %join_states.1 = (f32[256,4096]{1,0:T(8,128)}, f32[8,256]{1,0:T(8,128)}) custom-call(s32[1]{0:T(128)} %bitcast.place, bf16[256,4096]{1,0:T(8,128)(2,1)} %queries.5, f32[256,4096]{1,0:T(8,128)} %intra.1.inside, f32[32,256]{1,0:T(8,128)} %get-tuple-element.26.running, bf16[512,128]{1,0:T(8,128)(2,1)} %get-tuple-element.35.refs_0_, ...), custom_call_target="tpu_custom_call" | custom-call | bytes 25830000 | tf_op jit(solution)/shard_map/join_states/pallas_call | solution.py:301
  119.1 5.5 %all-to-all-start = ((bf16[16,2,128,128]{3,2,1,0:T(8,128)(2,1)}), bf16[16,2,128,128]{3,2,1,0:T(8,128)(2,1)}, u32[]{:S(2)}, u32[]{:S(2)}) async-start(bf16[16,2,128,128]{3,2,1,0:T(8,128)(2,1)} %get-tuple-element.46), calls=%async_computation | async-start | bytes 2097152 | tf_op jit(solution)/shard_map/all_to_all | solution.py:570
  124.6 0.1 copy.22
  124.6 0.1 reshape.30
  124.8 9.2 %collective-permute-start.15 = (f32[8,256]{1,0:T(8,128)S(1)}, f32[8,256]{1,0:T(8,128)S(1)}, u32[]{:S(2)}, u32[]{:S(2)}) collective-permute-start(f32[8,256]{1,0:T(8,128)S(1)} %copy-done.18), channel_id=1, source_target_pairs={{0,1},{1,0},{2,3},{3,2},{4,5},{5,4},{6,7},{7,6},{8,9},{9,8},{10,11... | collective-permute-start | bytes 24584 | tf_op jit(solution)/shard_map/ppermute | solution.py:577
  134.0 0.5 fusion.6.counts
  134.5 0.6 reshape.29.owners
  135.1 0.6 copy-done.19
  135.7 5.4 %gated_norm.1 = bf16[256,4096]{1,0:T(8,128)(2,1)} custom-call(f32[256,4096]{1,0:T(8,128)} %get-tuple-element.44.attn, bf16[256,4096]{1,0:T(8,128)(2,1)} %gate.1, f32[1,4096]{1,0:T(1,128)} %bitcast.8, f32[8,256]{1,0:T(8,128)} %get-tuple-element.45.refs_0_, f32[8,256]{1,0:T(8,128)} %copy-done.19), custom_call_target="tpu_custom_call" | custom-call | bytes 22140000 | tf_op jit(solution)/shard_map/gated_norm/pallas_call | solution.py:339
  141.1 38.6 %soft_attention.2.refs_0_ = bf16[256,4096]{1,0:T(8,128)(2,1)} custom-call(s32[32]{0:T(128)} %reshape.29.owners, s32[2]{0:T(128)} %fusion.6.counts, bf16[256,4096]{1,0:T(8,128)(2,1)} %queries.7, bf16[256,512]{1,0:T(8,128)(2,1)} %slab_k.3, bf16[256,512]{1,0:T(8,128)(2,1)} %slab_v.3, bf16[16,2,128,384]{3,2,1,0:T(8,128)(2,1)} %copy-done), custom_call_target="tpu_custom_call" | custom-call | bytes 99630000 | tf_op jit(solution)/shard_map/soft_attention/pallas_call | solution.py:497
  179.8 14.6 %soft_attention.3 = bf16[256,4096]{1,0:T(8,128)(2,1)} custom-call(s32[32]{0:T(128)} %reshape.29.owners, s32[2]{0:T(128)} %fusion.6.counts, bf16[256,4096]{1,0:T(8,128)(2,1)} %queries.7, bf16[256,512]{1,0:T(8,128)(2,1)} %slab_k.3, bf16[256,512]{1,0:T(8,128)(2,1)} %slab_v.3, ...), custom_call_target="tpu_custom_call", output_to_operand_aliasing={{}: (6, {})} | custom-call | bytes 33210000 | tf_op jit(solution)/shard_map/soft_attention/pallas_call | solution.py:497
  (50 shorter events, 0.2 us)
Async XLA Ops:
  6.9 6.5 %copy-start.16 = (f32[256,32]{0,1:T(8,128)S(1)}, f32[256,32]{0,1:T(8,128)}, u32[]{:S(2)}) copy-start(f32[256,32]{0,1:T(8,128)} %param.16) | copy-start | bytes 98308
  6.9 112.2 %all-to-all-start.1 = ((bf16[16,2,128,384]{3,2,1,0:T(8,128)(2,1)}), bf16[16,2,128,384]{3,2,1,0:T(8,128)(2,1)S(1)}, u32[]{:S(2)}, u32[]{:S(2)}) async-start(bf16[16,2,128,384]{3,2,1,0:T(8,128)(2,1)} %get-tuple-element.47), calls=%async_computation.1 | async-start | bytes 6291456 | tf_op jit(solution)/shard_map/all_to_all | solution.py:567
  19.6 13.4 %collective-permute-start = (bf16[528,128]{1,0:T(8,128)(2,1)}, bf16[528,128]{1,0:T(8,128)(2,1)S(1)}, u32[]{:S(2)}, u32[]{:S(2)}) collective-permute-start(bf16[528,128]{1,0:T(8,128)(2,1)} %get-tuple-element.28), channel_id=1, source_target_pairs={{0,2},{2,0},{4,6},{6,4},{8,10},{10,8},{12,14},{14,12},{16,18},{18,... | collective-permute-start | bytes 405512 | tf_op jit(solution)/shard_map/ppermute | solution.py:355
  20.8 21.3 %collective-permute-start.1 = (bf16[528,128]{1,0:T(8,128)(2,1)}, bf16[528,128]{1,0:T(8,128)(2,1)S(1)}, u32[]{:S(2)}, u32[]{:S(2)}) collective-permute-start(bf16[528,128]{1,0:T(8,128)(2,1)} %get-tuple-element.29), channel_id=1, source_target_pairs={{0,4},{2,6},{4,0},{6,2},{8,12},{10,14},{12,8},{14,10},{16,20},{18,... | collective-permute-start | bytes 405512 | tf_op jit(solution)/shard_map/ppermute | solution.py:355
  22.0 20.1 %collective-permute-start.2 = (bf16[528,128]{1,0:T(8,128)(2,1)}, bf16[528,128]{1,0:T(8,128)(2,1)S(1)}, u32[]{:S(2)}, u32[]{:S(2)}) collective-permute-start(bf16[528,128]{1,0:T(8,128)(2,1)} %get-tuple-element.30), channel_id=1, source_target_pairs={{0,6},{2,4},{4,2},{6,0},{8,14},{10,12},{12,10},{14,8},{16,22},{18,... | collective-permute-start | bytes 405512 | tf_op jit(solution)/shard_map/ppermute | solution.py:355
  22.3 45.0 %collective-permute-start.3 = (bf16[528,128]{1,0:T(8,128)(2,1)}, bf16[528,128]{1,0:T(8,128)(2,1)S(1)}, u32[]{:S(2)}, u32[]{:S(2)}) collective-permute-start(bf16[528,128]{1,0:T(8,128)(2,1)} %get-tuple-element.31), channel_id=1, source_target_pairs={{0,8},{2,10},{4,12},{6,14},{8,0},{10,2},{12,4},{14,6},{16,24},{18,... | collective-permute-start | bytes 405512 | tf_op jit(solution)/shard_map/ppermute | solution.py:355
  22.6 47.7 %collective-permute-start.4 = (bf16[528,128]{1,0:T(8,128)(2,1)}, bf16[528,128]{1,0:T(8,128)(2,1)S(1)}, u32[]{:S(2)}, u32[]{:S(2)}) collective-permute-start(bf16[528,128]{1,0:T(8,128)(2,1)} %get-tuple-element.32), channel_id=1, source_target_pairs={{0,10},{2,8},{4,14},{6,12},{8,2},{10,0},{12,6},{14,4},{16,26},{18,... | collective-permute-start | bytes 405512 | tf_op jit(solution)/shard_map/ppermute | solution.py:355
  33.0 43.0 %copy-start.1 = (bf16[528,128]{1,0:T(8,128)(2,1)}, bf16[528,128]{1,0:T(8,128)(2,1)S(1)}, u32[]{:S(2)}) copy-start(bf16[528,128]{1,0:T(8,128)(2,1)S(1)} %collective-permute-done.refs_1_) | copy-start | bytes 405508
  33.0 40.1 %collective-permute-start.5 = (bf16[528,128]{1,0:T(8,128)(2,1)}, bf16[528,128]{1,0:T(8,128)(2,1)S(1)}, u32[]{:S(2)}, u32[]{:S(2)}) collective-permute-start(bf16[528,128]{1,0:T(8,128)(2,1)} %get-tuple-element.33), channel_id=1, source_target_pairs={{0,12},{2,14},{4,8},{6,10},{8,4},{10,6},{12,0},{14,2},{16,28},{18,... | collective-permute-start | bytes 405512 | tf_op jit(solution)/shard_map/ppermute | solution.py:355
  42.1 33.9 %copy-start.2 = (bf16[528,128]{1,0:T(8,128)(2,1)}, bf16[528,128]{1,0:T(8,128)(2,1)S(1)}, u32[]{:S(2)}) copy-start(bf16[528,128]{1,0:T(8,128)(2,1)S(1)} %collective-permute-done.1.refs_2_) | copy-start | bytes 405508
  42.1 33.9 %collective-permute-start.6 = (bf16[528,128]{1,0:T(8,128)(2,1)}, bf16[528,128]{1,0:T(8,128)(2,1)S(1)}, u32[]{:S(2)}, u32[]{:S(2)}) collective-permute-start(bf16[528,128]{1,0:T(8,128)(2,1)} %get-tuple-element.34), channel_id=1, source_target_pairs={{0,14},{2,12},{4,10},{6,8},{8,6},{10,4},{12,2},{14,0},{16,30},{18,... | collective-permute-start | bytes 405512 | tf_op jit(solution)/shard_map/ppermute | solution.py:355
  42.1 33.9 %copy-start.3 = (bf16[528,128]{1,0:T(8,128)(2,1)}, bf16[528,128]{1,0:T(8,128)(2,1)S(1)}, u32[]{:S(2)}) copy-start(bf16[528,128]{1,0:T(8,128)(2,1)S(1)} %collective-permute-done.2.refs_3_) | copy-start | bytes 405508
  67.3 8.7 %copy-start.4 = (bf16[528,128]{1,0:T(8,128)(2,1)}, bf16[528,128]{1,0:T(8,128)(2,1)S(1)}, u32[]{:S(2)}) copy-start(bf16[528,128]{1,0:T(8,128)(2,1)S(1)} %collective-permute-done.3.refs_4_) | copy-start | bytes 405508
  70.2 5.8 %copy-start.5 = (bf16[528,128]{1,0:T(8,128)(2,1)}, bf16[528,128]{1,0:T(8,128)(2,1)S(1)}, u32[]{:S(2)}) copy-start(bf16[528,128]{1,0:T(8,128)(2,1)S(1)} %collective-permute-done.4.refs_5_) | copy-start | bytes 405508
  73.1 2.9 %copy-start.6 = (bf16[528,128]{1,0:T(8,128)(2,1)}, bf16[528,128]{1,0:T(8,128)(2,1)S(1)}, u32[]{:S(2)}) copy-start(bf16[528,128]{1,0:T(8,128)(2,1)S(1)} %collective-permute-done.5.refs_6_) | copy-start | bytes 405508
  76.0 0.7 copy-start.7
  78.9 11.5 %collective-permute-start.7 = (bf16[512,128]{1,0:T(8,128)(2,1)}, bf16[512,128]{1,0:T(8,128)(2,1)S(1)}, u32[]{:S(2)}, u32[]{:S(2)}) collective-permute-start(bf16[512,128]{1,0:T(8,128)(2,1)} %walk_states.2), channel_id=1, source_target_pairs={{0,16},{2,18},{4,20},{6,22},{8,24},{10,26},{12,28},{14,30},{1,17},... | collective-permute-start | bytes 393224 | tf_op jit(solution)/shard_map/ppermute | solution.py:364
  90.4 0.6 copy-start.8
  93.7 4.9 %collective-permute-start.10 = (bf16[512,128]{1,0:T(8,128)(2,1)}, bf16[512,128]{1,0:T(8,128)(2,1)S(1)}, u32[]{:S(2)}, u32[]{:S(2)}) collective-permute-start(bf16[512,128]{1,0:T(8,128)(2,1)} %get-tuple-element.38), channel_id=1, source_target_pairs={{0,6},{2,4},{4,2},{6,0},{8,14},{10,12},{12,10},{14,8},{16,22},{18,... | collective-permute-start | bytes 393224 | tf_op jit(solution)/shard_map/ppermute | solution.py:355
  93.7 6.1 %collective-permute-start.11 = (bf16[512,128]{1,0:T(8,128)(2,1)}, bf16[512,128]{1,0:T(8,128)(2,1)S(1)}, u32[]{:S(2)}, u32[]{:S(2)}) collective-permute-start(bf16[512,128]{1,0:T(8,128)(2,1)} %get-tuple-element.39), channel_id=1, source_target_pairs={{0,8},{2,10},{4,12},{6,14},{8,0},{10,2},{12,4},{14,6},{16,24},{18,... | collective-permute-start | bytes 393224 | tf_op jit(solution)/shard_map/ppermute | solution.py:355
  94.6 16.5 %collective-permute-start.12 = (bf16[512,128]{1,0:T(8,128)(2,1)}, bf16[512,128]{1,0:T(8,128)(2,1)S(1)}, u32[]{:S(2)}, u32[]{:S(2)}) collective-permute-start(bf16[512,128]{1,0:T(8,128)(2,1)} %get-tuple-element.40), channel_id=1, source_target_pairs={{0,10},{2,8},{4,14},{6,12},{8,2},{10,0},{12,6},{14,4},{16,26},{18,... | collective-permute-start | bytes 393224 | tf_op jit(solution)/shard_map/ppermute | solution.py:355
  96.1 14.9 %collective-permute-start.13 = (bf16[512,128]{1,0:T(8,128)(2,1)}, bf16[512,128]{1,0:T(8,128)(2,1)S(1)}, u32[]{:S(2)}, u32[]{:S(2)}) collective-permute-start(bf16[512,128]{1,0:T(8,128)(2,1)} %get-tuple-element.41), channel_id=1, source_target_pairs={{0,12},{2,14},{4,8},{6,10},{8,4},{10,6},{12,0},{14,2},{16,28},{18,... | collective-permute-start | bytes 393224 | tf_op jit(solution)/shard_map/ppermute | solution.py:355
  97.3 13.8 %collective-permute-start.14 = (bf16[512,128]{1,0:T(8,128)(2,1)}, bf16[512,128]{1,0:T(8,128)(2,1)S(1)}, u32[]{:S(2)}, u32[]{:S(2)}) collective-permute-start(bf16[512,128]{1,0:T(8,128)(2,1)} %get-tuple-element.42), channel_id=1, source_target_pairs={{0,14},{2,12},{4,10},{6,8},{8,6},{10,4},{12,2},{14,0},{16,30},{18,... | collective-permute-start | bytes 393224 | tf_op jit(solution)/shard_map/ppermute | solution.py:355
  98.6 12.4 %copy-start.9 = (bf16[512,128]{1,0:T(8,128)(2,1)}, bf16[512,128]{1,0:T(8,128)(2,1)S(1)}, u32[]{:S(2)}) copy-start(bf16[512,128]{1,0:T(8,128)(2,1)S(1)} %collective-permute-done.10.refs_3_) | copy-start | bytes 393220
  98.6 12.4 %collective-permute-start.8 = (bf16[512,128]{1,0:T(8,128)(2,1)}, bf16[512,128]{1,0:T(8,128)(2,1)S(1)}, u32[]{:S(2)}, u32[]{:S(2)}) collective-permute-start(bf16[512,128]{1,0:T(8,128)(2,1)} %get-tuple-element.36), channel_id=1, source_target_pairs={{0,2},{2,0},{4,6},{6,4},{8,10},{10,8},{12,14},{14,12},{16,18},{18,... | collective-permute-start | bytes 393224 | tf_op jit(solution)/shard_map/ppermute | solution.py:355
  99.8 11.2 %copy-start.10 = (bf16[512,128]{1,0:T(8,128)(2,1)}, bf16[512,128]{1,0:T(8,128)(2,1)S(1)}, u32[]{:S(2)}) copy-start(bf16[512,128]{1,0:T(8,128)(2,1)S(1)} %collective-permute-done.11.refs_4_) | copy-start | bytes 393220
  99.8 11.3 %collective-permute-start.9 = (bf16[512,128]{1,0:T(8,128)(2,1)}, bf16[512,128]{1,0:T(8,128)(2,1)S(1)}, u32[]{:S(2)}, u32[]{:S(2)}) collective-permute-start(bf16[512,128]{1,0:T(8,128)(2,1)} %get-tuple-element.37), channel_id=1, source_target_pairs={{0,4},{2,6},{4,0},{6,2},{8,12},{10,14},{12,8},{14,10},{16,20},{18,... | collective-permute-start | bytes 393224 | tf_op jit(solution)/shard_map/ppermute | solution.py:355
  111.0 0.7 copy-start.11
  111.1 0.7 copy-start.12
  111.1 0.7 copy-start.13
  111.1 0.7 copy-start.14
  111.1 0.7 copy-start.15
  119.0 5.5 %copy-start.17 = (s32[32,16]{0,1:T(8,128)S(1)}, s32[32,16]{0,1:T(8,128)}, u32[]{:S(2)}) copy-start(s32[32,16]{0,1:T(8,128)} %param.24) | copy-start | bytes 6148
  119.0 5.6 %copy-start.20 = (s32[32]{0:T(128)S(1)}, s32[32]{0:T(128)}, u32[]{:S(2)}) copy-start(s32[32]{0:T(128)} %param.25) | copy-start | bytes 388
  119.0 5.7 %copy-start.18 = (f32[8,256]{1,0:T(8,128)S(1)}, f32[8,256]{1,0:T(8,128)}, u32[]{:S(2)}) copy-start(f32[8,256]{1,0:T(8,128)} %get-tuple-element.45.refs_0_) | copy-start | bytes 24580
  119.1 22.0 %copy-start = (bf16[16,2,128,384]{3,2,1,0:T(8,128)(2,1)}, bf16[16,2,128,384]{3,2,1,0:T(8,128)(2,1)S(1)}, u32[]{:S(2)}) copy-start(bf16[16,2,128,384]{3,2,1,0:T(8,128)(2,1)S(1)} %all-to-all-done.1.arrived) | copy-start | bytes 9437188
  119.1 60.7 %all-to-all-start = ((bf16[16,2,128,128]{3,2,1,0:T(8,128)(2,1)}), bf16[16,2,128,128]{3,2,1,0:T(8,128)(2,1)}, u32[]{:S(2)}, u32[]{:S(2)}) async-start(bf16[16,2,128,128]{3,2,1,0:T(8,128)(2,1)} %get-tuple-element.46), calls=%async_computation | async-start | bytes 2097152 | tf_op jit(solution)/shard_map/all_to_all | solution.py:570
  124.8 10.3 %collective-permute-start.15 = (f32[8,256]{1,0:T(8,128)S(1)}, f32[8,256]{1,0:T(8,128)S(1)}, u32[]{:S(2)}, u32[]{:S(2)}) collective-permute-start(f32[8,256]{1,0:T(8,128)S(1)} %copy-done.18), channel_id=1, source_target_pairs={{0,1},{1,0},{2,3},{3,2},{4,5},{5,4},{6,7},{7,6},{8,9},{9,8},{10,11... | collective-permute-start | bytes 24584 | tf_op jit(solution)/shard_map/ppermute | solution.py:577
  135.1 0.6 copy-start.19

commit v2 on v1

--- a/solution.py
+++ b/solution.py
@@ -11,12 +11,26 @@
 HD = 128
 BLOCK = 128
 STEP_HEADS = 8
-PAD = 16
+GROUP = 4
 VMEM_LIMIT = 56 * 1024 * 1024
 F32 = jnp.float32
 BF16 = jnp.bfloat16
 NT = (((1,), (1,)), ((), ()))
-TN = (((0,), (0,)), ((), ()))
+NN = (((1,), (0,)), ((), ()))
+
+
+def tail_rows(per):
+    return -(-3 * per // 16) * 16
+
+
+def split_logs(logs):
+    high = logs.astype(BF16).astype(F32)
+    middle = (logs - high).astype(BF16).astype(F32)
+    rows = [high, middle, logs - high - middle]
+    spare = tail_rows(logs.shape[0]) - 3 * logs.shape[0]
+    if spare:
+        rows.append(jnp.zeros((spare, HD), F32))
+    return jnp.concatenate(rows, axis=0).astype(BF16)
 
 
 def params(**more):
@@ -81,7 +95,7 @@
     step = pl.program_id(0)
     rows = keys.shape[0]
     mine = place[0]
-    per = hold.shape[1] // HD
+    per = running.shape[0] // group
 
     @pl.when(step == 0)
     def _():
@@ -90,7 +104,7 @@
         running[...] = lax.dot_general(
             decay[...],
             (s <= t).astype(F32),
-            TN,
+            NN,
             precision=lax.Precision.HIGHEST,
             preferred_element_type=F32,
         )
@@ -99,10 +113,7 @@
     running_out[...] = here
     total = here[:, rows - 1 : rows]
     fade = jnp.exp(total - here)
-    wide = jnp.broadcast_to(total, (STEP_HEADS, HD))
-    high = wide.astype(BF16).astype(F32)
-    middle = (wide - high).astype(BF16).astype(F32)
-    low = wide - high - middle
+    logs = jnp.broadcast_to(total, (STEP_HEADS, HD))
     for dest in range(STEP_HEADS // per):
         slot = (step * (STEP_HEADS // per) + dest) ^ mine
         for i in range(per):
@@ -115,11 +126,7 @@
                 preferred_element_type=F32,
             )
             hold[slot, i * HD : (i + 1) * HD, :] = state.astype(BF16)
-        mine_rows = slice(dest * per, (dest + 1) * per)
-        tail = [high[mine_rows], middle[mine_rows], low[mine_rows]]
-        if 3 * per < PAD:
-            tail.append(jnp.zeros((PAD - 3 * per, HD), F32))
-        hold[slot, per * HD :, :] = jnp.concatenate(tail, axis=0).astype(BF16)
+        hold[slot, per * HD :, :] = split_logs(logs[dest * per : (dest + 1) * per])
 
     @pl.when(step == pl.num_programs(0) - 1)
     def _():
@@ -128,9 +135,9 @@
 
 
 def segment_states(keys, values, decay, place, group):
-    rows, heads = decay.shape
+    heads, rows = decay.shape
     per = heads // group
-    size = per * HD + PAD
+    size = per * HD + tail_rows(per)
     wide = STEP_HEADS * HD
     return pl.pallas_call(
         functools.partial(state_kernel, group),
@@ -142,7 +149,7 @@
             in_specs=[
                 pl.BlockSpec((rows, wide), lambda i, _: (0, i)),
                 pl.BlockSpec((rows, wide), lambda i, _: (0, i)),
-                pl.BlockSpec((rows, heads), lambda i, _: (0, 0)),
+                pl.BlockSpec((heads, rows), lambda i, _: (0, 0)),
             ],
             out_specs=[pl.BlockSpec((STEP_HEADS, rows), lambda i, _: (i, 0))]
             + [pl.BlockSpec((size, HD), lambda i, _: (0, 0))] * group,
@@ -197,63 +204,69 @@
     )(queries, keys, values, running)
 
 
-def read_total(message, per, head):
-    base = per * HD + head
-    rows = [message[base + k * per : base + k * per + 1, :].astype(F32) for k in range(3)]
-    return rows[0] + rows[1] + rows[2]
-
-
-def walk_kernel(group, per, with_start, place, *refs):
-    arrived = refs[:group]
-    mine = place[0]
-    if with_start:
-        start, outs, hold = refs[group], refs[group + 1 : -1], refs[-1]
-    else:
-        outs, hold = refs[group:-1], refs[-1]
+def read_logs(message, per):
+    tail = message[per * HD :, :].astype(F32)
+    return tail[:per] + tail[per : 2 * per] + tail[2 * per : 3 * per]
+
+
+def total_kernel(group, per, place, *refs):
+    arrived, out, hold = refs[:group], refs[group], refs[group + 1]
     for k in range(group):
-        hold[mine ^ k] = arrived[k][...]
+        hold[place[0] ^ k] = arrived[k][...]
+    logs = [read_logs(hold.at[j], per) for j in range(group)]
+    fades = [jnp.exp(log) for log in logs]
     for head in range(per):
         rows = slice(head * HD, (head + 1) * HD)
-        if with_start:
-            state = start[rows, :].astype(F32)
-        else:
-            state = jnp.zeros((HD, HD), F32)
+        state = hold[0, rows, :].astype(F32)
+        for j in range(1, group):
+            state = fades[j][head : head + 1, :] * state + hold[j, rows, :].astype(F32)
+        out[rows, :] = state.astype(BF16)
+    out[per * HD :, :] = split_logs(functools.reduce(lambda x, y: x + y, logs))
+
+
+def enter_kernel(group, per, place, *refs):
+    arrived, earlier, refs = refs[:group], refs[group : -group - 1], refs[-group - 1 :]
+    outs, hold = refs[:-1], refs[-1]
+    for k in range(group):
+        hold[place[0] ^ k] = arrived[k][...]
+    fades = [jnp.exp(read_logs(hold.at[j], per)) for j in range(group)]
+    passed = [jnp.exp(read_logs(message, per)) for message in earlier]
+    for head in range(per):
+        rows = slice(head * HD, (head + 1) * HD)
+        state = jnp.zeros((HD, HD), F32)
+        for message, fade in zip(earlier, passed):
+            state = fade[head : head + 1, :] * state + message[rows, :].astype(F32)
         for j in range(group):
-            message = hold.at[j]
-            own = message[rows, :].astype(F32)
-            fade = jnp.exp(read_total(message[...], per, head))
-            if with_start:
-                hold[j, rows, :] = state.astype(BF16)
-            state = fade * state + own
-        if not with_start:
-            outs[0][rows, :] = state.astype(outs[0].dtype)
-    if with_start:
-        for k in range(group):
-            outs[k][...] = hold[mine ^ k, : per * HD, :]
-
-
-def walk(arrived, place, start=None):
+            own = hold[j, rows, :].astype(F32)
+            hold[j, rows, :] = state.astype(BF16)
+            state = fades[j][head : head + 1, :] * state + own
+    for k in range(group):
+        outs[k][...] = hold[place[0] ^ k, : per * HD, :]
+
+
+def walk(kernel, arrived, earlier, place, per):
     group = len(arrived)
     size = arrived[0].shape[0]
-    per = (size - PAD) // HD
-    whole = pl.BlockSpec((size, HD), lambda i, _: (0, 0))
-    part = pl.BlockSpec((per * HD, HD), lambda i, _: (0, 0))
-    with_start = start is not None
-    outs = group if with_start else 1
+    message = pl.BlockSpec((size, HD), lambda i, _: (0, 0))
+    state = pl.BlockSpec((per * HD, HD), lambda i, _: (0, 0))
+    out_shape, out_specs = jax.ShapeDtypeStruct((size, HD), BF16), message
+    if kernel is enter_kernel:
+        out_shape = [jax.ShapeDtypeStruct((per * HD, HD), BF16)] * group
+        out_specs = [state] * group
     return pl.pallas_call(
-        functools.partial(walk_kernel, group, per, with_start),
-        out_shape=[jax.ShapeDtypeStruct((per * HD, HD), BF16)] * outs,
+        functools.partial(kernel, group, per),
+        out_shape=out_shape,
         grid_spec=pltpu.PrefetchScalarGridSpec(
             num_scalar_prefetch=1,
             grid=(1,),
-            in_specs=[whole] * group + [part] * with_start,
-            out_specs=[part] * outs,
+            in_specs=[message] * (group + len(earlier)),
+            out_specs=out_specs,
             scratch_shapes=[pltpu.VMEM((group, size, HD), BF16)],
         ),
         compiler_params=params(),
         cost_estimate=cost(2.5),
         name="walk_states",
-    )(place, *arrived, *((start,) if with_start else ()))
+    )(place, *arrived, *earlier)
 
 
 def join_kernel(group, place, queries, inside, running, *refs):
@@ -356,114 +369,99 @@
     ]
 
 
-def states_before_group(total, logs, group):
+def groups_before(total, group):
     n = lax.axis_size("ctx")
-    groups = n // group
-
-    def shift(array, by):
-        return lax.ppermute(
-            array, "ctx", [(i, i + by * group) for i in range(n - by * group)]
-        )
-
-    before = shift(total, 1)
-    if groups == 2:
-        return before
-    span = shift(logs, 1)
-    reach = 1
-    while reach < groups - 1:
-        far = shift(before, reach).astype(F32)
-        before = (
-            far * jnp.exp(span)[:, None] + before.astype(F32)
-        ).astype(BF16)
-        span = span + shift(span, reach)
-        reach *= 2
-    return before
-
-
-def soft_kernel(
-    chosen, owners, counts, queries, slab_k, slab_v, arrived, *refs
-):
-    out, scores, top, weight_sum, mixed = refs[-5:]
+    return [
+        lax.ppermute(total, "ctx", [(i, i + by) for i in range(n - by)])
+        for by in range(n - group, 0, -group)
+    ]
+
+
+def soft_kernel(chosen, owners, counts, queries, slab_k, slab_v, arrived, *refs):
+    out, top, weight_sum, mixed = refs[-4:]
     b = pl.program_id(1)
     count = counts[b]
     heads = queries.shape[1] // HD
-    chunk = 2 * BLOCK
-    chunks = heads * BLOCK // chunk
+    rows = min(4, heads) * BLOCK
+    chunks = heads * BLOCK // rows
     scale = math.log2(math.e) / math.sqrt(HD)
-    low = -1e30
-
-    def rows_of(r):
-        return jnp.concatenate(
-            [queries[:, (2 * r + i) * HD : (2 * r + i + 1) * HD] for i in range(2)], axis=0
-        )
-
-    def pair(kind, first, second):
-        return jnp.concatenate(
-            [
-                arrived[owners[b * chosen + first], kind],
-                arrived[owners[b * chosen + second], kind],
-            ],
-            axis=0,
-        )
-
-    def score(tile, k, allowed, first):
-        for r in range(chunks):
-            at = slice(r * chunk, (r + 1) * chunk)
-            s = lax.dot_general(rows_of(r), k, NT, preferred_element_type=F32)
-            if allowed is not None:
-                s = jnp.where(allowed, s, low)
-            scores[tile, at, :] = s
-            here = jnp.maximum(s[:, :BLOCK], s[:, BLOCK:])
-            top[at, :] = here if first else jnp.maximum(top[at, :], here)
-
-    t = lax.broadcasted_iota(jnp.int32, (chunk, chunk), 0) % BLOCK
-    s_at = lax.broadcasted_iota(jnp.int32, (chunk, chunk), 1)
-    score(0, slab_k[...], s_at <= t + b * BLOCK, True)
-    pairs = count // 2
-
-    def score_pair(p, _):
-        score(p + 1, pair(0, 2 * p, 2 * p + 1), None, False)
-        return 0
-
-    lax.fori_loop(0, pairs, score_pair, 0)
-    odd = count % 2 == 1
-
-    @pl.when(odd)
-    def _():
-        score(pairs + 1, pair(0, count - 1, count - 1), s_at < BLOCK, False)
-
-    for r in range(chunks):
-        at = slice(r * chunk, (r + 1) * chunk)
-        highest = jnp.max(top[at, :], axis=1, keepdims=True) * scale
-        top[at, :] = jnp.broadcast_to(highest, (chunk, BLOCK))
-
-    def mix(tile, v, first):
-        for r in range(chunks):
-            at = slice(r * chunk, (r + 1) * chunk)
-            highest = top[at, :]
-            left = jnp.exp2(scores[tile, at, :BLOCK] * scale - highest)
-            right = jnp.exp2(scores[tile, at, BLOCK:] * scale - highest)
-            w = jnp.concatenate([left.astype(BF16), right.astype(BF16)], axis=1)
-            more = jnp.dot(w, v, preferred_element_type=F32)
-            if first:
-                weight_sum[at, :] = left + right
-                mixed[at, :] = more
-            else:
-                weight_sum[at, :] += left + right
-                mixed[at, :] += more
-
-    mix(0, slab_v[...], True)
-
-    def mix_pair(p, _):
-        mix(p + 1, pair(1, 2 * p, 2 * p + 1), False)
-        return 0
-
-    lax.fori_loop(0, pairs, mix_pair, 0)
-
-    @pl.when(odd)
-    def _():
-        mix(pairs + 1, pair(1, count - 1, count - 1), False)
-
+
+    def spans():
+        return [(r, slice(r * rows, (r + 1) * rows)) for r in range(chunks)]
+
+    def queries_of(r):
+        per = rows // BLOCK
+        parts = [queries[:, (per * r + i) * HD : (per * r + i + 1) * HD] for i in range(per)]
+        return jnp.concatenate(parts, axis=0)
+
+    def fetch(kind, first, number):
+        parts = [arrived[owners[b * chosen + first + i], kind] for i in range(number)]
+        return parts[0] if number == 1 else jnp.concatenate(parts, axis=0)
+
+    t = lax.broadcasted_iota(jnp.int32, (rows, slab_k.shape[0]), 0) % BLOCK
+    s_at = lax.broadcasted_iota(jnp.int32, (rows, slab_k.shape[0]), 1)
+    causal = s_at <= t + b * BLOCK
+
+    def weigh(scores, highest):
+        number = scores.shape[1] // BLOCK
+        parts = [
+            jnp.exp2(scores[:, i * BLOCK : (i + 1) * BLOCK] * scale - highest)
+            for i in range(number)
+        ]
+        summed = functools.reduce(lambda x, y: x + y, parts)
+        parts = [part.astype(BF16) for part in parts]
+        return summed, parts[0] if number == 1 else jnp.concatenate(parts, axis=1)
+
+    def cached(first, number):
+        k, v = fetch(0, first, number), fetch(1, first, number)
+        for r, at in spans():
+            scores = lax.dot_general(queries_of(r), k, NT, preferred_element_type=F32)
+            summed, w = weigh(scores, top[at, :])
+            weight_sum[at, :] += summed
+            mixed[at, :] += jnp.dot(w, v, preferred_element_type=F32)
+
+    def raise_top(j):
+        k = fetch(0, j, 1)
+        for r, at in spans():
+            scores = lax.dot_general(queries_of(r), k, NT, preferred_element_type=F32)
+            here = jnp.max(scores, axis=1, keepdims=True) * scale
+            top[at, :] = jnp.maximum(top[at, :], here)
+
+    def attempt(again):
+        for r, at in spans():
+            scores = lax.dot_general(queries_of(r), slab_k[...], NT, preferred_element_type=F32)
+            scores = jnp.where(causal, scores, -1e30)
+            highest = jnp.max(scores, axis=1, keepdims=True) * scale
+            top[at, :] = jnp.maximum(top[at, :], highest)
+            summed, w = weigh(scores, top[at, :])
+            weight_sum[at, :] = summed
+            mixed[at, :] = jnp.dot(w, slab_v[...], preferred_element_type=F32)
+
+        def eight(p, carry):
+            cached(8 * p, 8)
+            return carry
+
+        lax.fori_loop(0, count // 8, eight, 0)
+        for number in (4, 2, 1):
+
+            @pl.when((count // number) % 2 == 1)
+            def _(number=number):
+                cached((count // (2 * number)) * (2 * number), number)
+
+        fine = jnp.max(weight_sum[...]) < 1e25
+
+        @pl.when(jnp.logical_not(fine))
+        def _():
+            def turn(j, carry):
+                raise_top(j)
+                return carry
+
+            lax.fori_loop(0, count, turn, 0)
+
+        return jnp.logical_not(fine)
+
+    top[...] = jnp.full(top.shape, -1e30, F32)
+    lax.while_loop(lambda again: again, attempt, jnp.bool_(True))
     for head in range(heads):
         at = slice(head * BLOCK, (head + 1) * BLOCK)
         total = jnp.sum(weight_sum[at, :], axis=1, keepdims=True)
@@ -488,7 +486,6 @@
         + ([] if so_far is None else [pl.BlockSpec(memory_space=pl.ANY)]),
         out_specs=pl.BlockSpec((BLOCK, wide), lambda h, b, *_: (b, first + h)),
         scratch_shapes=[
-            pltpu.VMEM((chosen // 2 + 2, wide // HD * BLOCK, 2 * BLOCK), F32),
             pltpu.VMEM((wide // HD * BLOCK, BLOCK), F32),
             pltpu.VMEM((wide // HD * BLOCK, BLOCK), F32),
             pltpu.VMEM((wide // HD * BLOCK, BLOCK), F32),
@@ -500,13 +497,13 @@
         grid_spec=grid_spec,
         input_output_aliases={} if so_far is None else {6: 0},
         compiler_params=params(),
-        cost_estimate=cost(9 * kv_here),
+        cost_estimate=cost(8 * kv_here),
         name="soft_attention",
     )(owners, counts, queries, slab_k, slab_v, arrived, *(() if so_far is None else (so_far,)))
 
 
 def parts_of(kv_count):
-    return [kv_count] if kv_count < 2 else [kv_count - 1, 1]
+    return [kv_count - kv_count // 2, kv_count // 2] if kv_count > 1 else [1]
 
 
 def local(
@@ -533,7 +530,7 @@
     stored = cache_keys.shape[0] // BLOCK
     blocks_here = block_lists.shape[0] // n
     group = 1
-    while group < 8 and 2 * group <= n and heads % (2 * group) == 0:
+    while group < GROUP and 2 * group <= n and heads % (2 * group) == 0:
         group *= 2
     per = heads // group
 
@@ -546,28 +543,43 @@
     my_counts = lax.dynamic_slice_in_dim(counts, me, 1, 0).reshape(blocks_here)
     place = (me % group).reshape(1)
 
+    tied = lax.optimization_barrier
     parts = parts_of(kv_count)
-    outgoing = pack(spots, cache_keys, cache_values, 0, [part * HD for part in parts])
-
-    running, *messages = segment_states(lin_keys, lin_values, log_decay, place, group)
+    widths = [part * HD for part in parts]
+    outgoing = list(pack(spots, cache_keys, cache_values, 0, widths[:1]))
+    arrived = [lax.all_to_all(outgoing[0], "ctx", 0, 0, tiled=True)]
+
+    running, *messages = segment_states(lin_keys, lin_values, log_decay.T, place, group)
     messages = exchange_in_group(messages, group)
-    (total,) = walk(messages, place)
-    logs = None
-    if n // group > 2:
-        logs = sum(
-            message[per * HD : per * HD + 3 * per, 0].astype(F32).reshape(3, per).sum(0)
-            for message in messages
+    inside = intra(lin_queries, lin_keys, lin_values, running)
+    if len(parts) > 1:
+        outgoing += pack(spots, cache_keys, cache_values, widths[0], widths[1:])
+        inside, outgoing[1], messages[1] = tied((inside, outgoing[1], messages[1]))
+    total = walk(total_kernel, messages, (), place, per)
+    earlier = groups_before(total, group)
+    if len(parts) > 1:
+        block, arrived[0], *earlier = tied((outgoing[1], arrived[0], *earlier))
+        arrived.append(lax.all_to_all(block, "ctx", 0, 0, tiled=True))
+    states = exchange_in_group(walk(enter_kernel, messages, earlier, place, per), group)
+
+    def attend(i, so_far):
+        return soft_part(
+            my_owners,
+            my_counts,
+            soft_queries,
+            slab_keys,
+            slab_values,
+            arrived[i],
+            sum(parts[:i]),
+            chosen,
+            so_far,
         )
-        logs = jnp.repeat(logs, HD)
-    before = states_before_group(total, logs, group)
-    states = exchange_in_group(walk(messages, place, before), group)
-
-    inside = intra(lin_queries, lin_keys, lin_values, running)
+
+    soft_out = None
+    if len(parts) > 1:
+        soft_out = attend(0, None)
+        soft_out, running = tied((soft_out, running))
     attn, squares = join(lin_queries, inside, running, states, place)
-    arrived = [lax.all_to_all(outgoing[0], "ctx", 0, 0, tiled=True)]
-    for block in outgoing[1:]:
-        block, attn = lax.optimization_barrier((block, attn))
-        arrived.append(lax.all_to_all(block, "ctx", 0, 0, tiled=True))
     summands = [squares]
     reach = 1
     while reach < head_devices:
@@ -579,15 +591,9 @@
         reach *= 2
     features = head_devices * heads * HD
     lin_out = gated(attn, lin_gate, norm_gain, summands, features)
-
-    soft_out = None
-    first = 0
-    for part, block in zip(parts, arrived):
-        soft_out = soft_part(
-            my_owners, my_counts, soft_queries, slab_keys, slab_values, block, first, chosen, soft_out
-        )
-        first += part
-    return (lin_out, soft_out)
+    if len(parts) > 1:
+        lin_out, my_owners = tied((lin_out, my_owners))
+    return (lin_out, attend(len(parts) - 1, soft_out))
 
 
 def solution(mesh):

time: 195 us -> 225 us (1.15)
  the two profiles are of different devices: /device:TPU:25 before, /device:TPU:27 now
where the time goes in v2:
time: 225 us; the launch traced here: 223 us
  Pallas kernels  148 us (66%)
  waiting for transfers between devices  41 us (18%)
  starting transfers between devices  25.6 us (11%)
  local copies, waits for them, and re-layouts  6.39 us (3%)
    pallas_call x2, Pallas kernels, soft_part(): pl.pallas_call(functools.partial(soft_kernel, chosen), out_shape=jax.Shap...  107 us
    ppermute x3, waiting for transfers between devices, groups_before(): lax.ppermute(total, 'ctx', [(i, i + by) for i in range(n - by)])  28.4 us
    ppermute x6, waiting for transfers between devices, exchange_in_group(): lax.ppermute(messages[k], 'ctx', [(i, i ^ k) for i in range(n)])  11.5 us
    pallas_call x1, Pallas kernels, intra(): pl.pallas_call(intra_kernel, out_shape=jax.ShapeDtypeStruct((rows, featur...  9.93 us
    pallas_call x2, Pallas kernels, pack(): pl.pallas_call(functools.partial(pack_kernel, first), out_shape=[jax.Shap...  7.66 us
    pallas_call x1, Pallas kernels, join(): pl.pallas_call(functools.partial(join_kernel, group), out_shape=[jax.Shap...  7.13 us
    all_to_all x1, starting transfers between devices, local(): arrived.append(lax.all_to_all(block, 'ctx', 0, 0, tiled=True))  6.57 us
    all_to_all x1, starting transfers between devices, local(): arrived = [lax.all_to_all(outgoing[0], 'ctx', 0, 0, tiled=True)]  6.42 us
  transfers between devices with their start and end apart: 12, of which 4 were waited for; matrix products, arithmetic and copies ran while one was open for 1% of the time, Pallas kernels for 41%

profile of v2, /device:TPU:27, one launch (start us, length us, event | category | flops | bytes accessed | tf_op | source)
XLA Modules:
  0.0 222.9 jit_solution(13854720565699139548)
XLA Ops:
  0.6 0.7 fusion.2
  1.4 0.1 reduce_max.14
  1.4 0.7 reduce_max.18.spots
  2.2 3.8 %pack.3 = bf16[16,2,128,256]{3,2,1,0:T(8,128)(2,1)} custom-call(s32[16]{0:T(128)} %reduce_max.18.spots, bf16[1024,512]{1,0:T(8,128)(2,1)} %keys.7, bf16[1024,512]{1,0:T(8,128)(2,1)} %values.7), custom_call_target="tpu_custom_call" | custom-call | bytes 14760000 | tf_op jit(solution)/shard_map/pack/pallas_call | solution.py:77
  5.9 6.4 %all-to-all-start = ((bf16[16,2,128,256]{3,2,1,0:T(8,128)(2,1)}), bf16[16,2,128,256]{3,2,1,0:T(8,128)(2,1)S(1)}, u32[]{:S(2)}, u32[]{:S(2)}) async-start(bf16[16,2,128,256]{3,2,1,0:T(8,128)(2,1)} %pack.3), calls=%async_computation | async-start | bytes 4194304 | tf_op jit(solution)/shard_map/all_to_all | solution.py:550
  12.4 5.4 %segment_states.1 = (f32[32,256]{1,0:T(8,128)}, bf16[1056,128]{1,0:T(8,128)(2,1)}, bf16[1056,128]{1,0:T(8,128)(2,1)}, bf16[1056,128]{1,0:T(8,128)(2,1)}, bf16[1056,128]{1,0:T(8,128)(2,1)}) custom-call(s32[1]{0:T(128)} %bitcast.place, bf16[256,4096]{1,0:T(8,128)(2,1)} %keys.5, bf16[256,4096]{1,0:T(8,128)(2,1)} %values.5, f32[32,256]{1,0:T(8,128)} %bitcast.9), custom_call_target="tpu_custom_call" | custom-call | bytes 22140000 | tf_op jit(solution)/shard_map/segment_states/pallas_call | solution.py:142
  17.8 0.3 collective-permute-start
  18.1 1.2 collective-permute-start.1
  19.2 1.2 collective-permute-start.2
  20.4 3.9 %pack.2 = bf16[16,2,128,256]{3,2,1,0:T(8,128)(2,1)} custom-call(s32[16]{0:T(128)} %reduce_max.18.spots, bf16[1024,512]{1,0:T(8,128)(2,1)} %keys.7, bf16[1024,512]{1,0:T(8,128)(2,1)} %values.7), custom_call_target="tpu_custom_call" | custom-call | bytes 14760000 | tf_op jit(solution)/shard_map/pack/pallas_call | solution.py:77
  24.3 9.9 %intra.1.inside = f32[256,4096]{1,0:T(8,128)} custom-call(bf16[256,4096]{1,0:T(8,128)(2,1)} %queries.6, bf16[256,4096]{1,0:T(8,128)(2,1)} %keys.5, bf16[256,4096]{1,0:T(8,128)(2,1)} %values.5, f32[32,256]{1,0:T(8,128)} %get-tuple-element.34.running), custom_call_target="tpu_custom_call" | custom-call | bytes 36900000 | tf_op jit(solution)/shard_map/intra/pallas_call | solution.py:195
  34.2 0.0 collective-permute-done.refs_1_
  34.3 11.5 %collective-permute-done.1.refs_2_ = bf16[1056,128]{1,0:T(8,128)(2,1)S(1)} collective-permute-done((bf16[1056,128]{1,0:T(8,128)(2,1)}, bf16[1056,128]{1,0:T(8,128)(2,1)S(1)}, u32[]{:S(2)}, u32[]{:S(2)}) %collective-permute-start.1) | collective-permute-done | bytes 270368 | tf_op jit(solution)/shard_map/ppermute | solution.py:368
  45.8 0.0 collective-permute-done.2.refs_3_
  45.8 0.7 copy-done.3
  46.5 0.1 copy-done.4
  46.6 2.2 walk_states.2
  48.8 1.4 collective-permute-start.5
  50.2 1.3 collective-permute-start.4
  51.5 1.3 collective-permute-start.3
  52.8 9.3 %collective-permute-done.5.refs_6_ = bf16[1056,128]{1,0:T(8,128)(2,1)S(1)} collective-permute-done((bf16[1056,128]{1,0:T(8,128)(2,1)}, bf16[1056,128]{1,0:T(8,128)(2,1)S(1)}, u32[]{:S(2)}, u32[]{:S(2)}) %collective-permute-start.5) | collective-permute-done | bytes 270368 | tf_op jit(solution)/shard_map/ppermute | solution.py:375
  62.1 19.1 %collective-permute-done.4.refs_5_ = bf16[1056,128]{1,0:T(8,128)(2,1)S(1)} collective-permute-done((bf16[1056,128]{1,0:T(8,128)(2,1)}, bf16[1056,128]{1,0:T(8,128)(2,1)S(1)}, u32[]{:S(2)}, u32[]{:S(2)}) %collective-permute-start.4) | collective-permute-done | bytes 270368 | tf_op jit(solution)/shard_map/ppermute | solution.py:375
  81.2 0.0 collective-permute-done.3.refs_4_
  81.2 0.0 all-to-all-done.arrived
  81.2 0.0 copy-start.1
  81.2 1.3 copy-done.1
  82.6 6.6 %all-to-all-start.1 = ((bf16[16,2,128,256]{3,2,1,0:T(8,128)(2,1)}), bf16[16,2,128,256]{3,2,1,0:T(8,128)(2,1)S(1)}, u32[]{:S(2)}, u32[]{:S(2)}) async-start(bf16[16,2,128,256]{3,2,1,0:T(8,128)(2,1)} %pack.2), calls=%async_computation.1 | async-start | bytes 4194304 | tf_op jit(solution)/shard_map/all_to_all | solution.py:562
  89.1 0.1 copy.20
  89.3 2.9 %walk_states.3 = (bf16[1024,128]{1,0:T(8,128)(2,1)}, bf16[1024,128]{1,0:T(8,128)(2,1)}, bf16[1024,128]{1,0:T(8,128)(2,1)}, bf16[1024,128]{1,0:T(8,128)(2,1)}) custom-call(s32[1]{0:T(128)} %bitcast.place, bf16[1056,128]{1,0:T(8,128)(2,1)} %get-tuple-element.29.refs_0_, bf16[1056,128]{1,0:T(8,128)(2,1)} %copy-done.2, bf16[1056,128]{1,0:T(8,128)(2,1)} %copy-done.3, ...), custom_call_target="tpu_custom_call" | custom-call | bytes 9225000 | tf_op jit(solution)/shard_map/walk_states/pallas_call | solution.py:256
  92.2 0.3 collective-permute-start.6
  92.4 1.2 collective-permute-start.7
  93.6 1.2 collective-permute-start.8
  94.8 0.1 reshape.29
  94.9 0.6 reshape.28.owners
  95.6 0.6 fusion.6.counts
  96.2 53.5 %soft_attention.2.refs_0_ = bf16[256,4096]{1,0:T(8,128)(2,1)} custom-call(s32[32]{0:T(128)} %reshape.28.owners, s32[2]{0:T(128)} %fusion.6.counts, bf16[256,4096]{1,0:T(8,128)(2,1)} %queries.7, bf16[256,512]{1,0:T(8,128)(2,1)} %slab_k.3, bf16[256,512]{1,0:T(8,128)(2,1)} %slab_v.3, bf16[16,2,128,256]{3,2,1,0:T(8,128)(2,1)} %copy-done.1), custom_call_target="tpu_custom_call" | custom-call | bytes 59040000 | tf_op jit(solution)/shard_map/soft_attention/pallas_call | solution.py:494
  149.7 0.0 collective-permute-done.7.refs_2_
  149.7 0.7 copy-done.8
  150.4 0.1 copy-done.9
  150.5 0.1 copy-done.10
  150.5 7.1 %join_states.1 = (f32[256,4096]{1,0:T(8,128)}, f32[8,256]{1,0:T(8,128)}) custom-call(s32[1]{0:T(128)} %bitcast.place, bf16[256,4096]{1,0:T(8,128)(2,1)} %queries.6, f32[256,4096]{1,0:T(8,128)} %intra.1.inside, f32[32,256]{1,0:T(8,128)} %get-tuple-element.34.running, bf16[1024,128]{1,0:T(8,128)(2,1)} %get-tuple-element.38.refs_0_, ...), custom_call_target="tpu_custom_call" | custom-call | bytes 25830000 | tf_op jit(solution)/shard_map/join_states/pallas_call | solution.py:314
  157.7 3.3 %collective-permute-start.9 = (f32[8,256]{1,0:T(8,128)}, f32[8,256]{1,0:T(8,128)S(1)}, u32[]{:S(2)}, u32[]{:S(2)}) collective-permute-start(f32[8,256]{1,0:T(8,128)} %get-tuple-element.43.refs_0_), channel_id=1, source_target_pairs={{0,1},{1,0},{2,3},{3,2},{4,5},{5,4},{6,7},{7,6},{8,9},{9,8},{10,11... | collective-permute-start | bytes 24584 | tf_op jit(solution)/shard_map/ppermute | solution.py:589
  160.9 1.0 collective-permute-done.9.refs_1_
  161.9 0.6 copy-done.12
  162.5 5.4 %gated_norm.1 = bf16[256,4096]{1,0:T(8,128)(2,1)} custom-call(f32[256,4096]{1,0:T(8,128)} %get-tuple-element.42.attn, bf16[256,4096]{1,0:T(8,128)(2,1)} %gate.1, f32[1,4096]{1,0:T(1,128)} %bitcast.10, f32[8,256]{1,0:T(8,128)} %get-tuple-element.43.refs_0_, f32[8,256]{1,0:T(8,128)} %copy-done.12), custom_call_target="tpu_custom_call" | custom-call | bytes 22140000 | tf_op jit(solution)/shard_map/gated_norm/pallas_call | solution.py:352
  168.0 0.0 all-to-all-done.1.arrived
  168.0 1.3 copy-done
  169.3 53.6 %soft_attention.3 = bf16[256,4096]{1,0:T(8,128)(2,1)} custom-call(s32[32]{0:T(128)} %reshape.28.owners, s32[2]{0:T(128)} %fusion.6.counts, bf16[256,4096]{1,0:T(8,128)(2,1)} %queries.7, bf16[256,512]{1,0:T(8,128)(2,1)} %slab_k.3, bf16[256,512]{1,0:T(8,128)(2,1)} %slab_v.3, bf16[16,2,128,256]{3,2,1,0:T(8,128)(2,1)} %copy-done, ...), custom_call_target="tpu_custom_call", output_to_operand_aliasing={{}: (6, {})} | custom-call | bytes 59040000 | tf_op jit(solution)/shard_map/soft_attention/pallas_call | solution.py:494
  (24 shorter events, 0.1 us)
Async XLA Ops:
  5.9 75.3 %all-to-all-start = ((bf16[16,2,128,256]{3,2,1,0:T(8,128)(2,1)}), bf16[16,2,128,256]{3,2,1,0:T(8,128)(2,1)S(1)}, u32[]{:S(2)}, u32[]{:S(2)}) async-start(bf16[16,2,128,256]{3,2,1,0:T(8,128)(2,1)} %pack.3), calls=%async_computation | async-start | bytes 4194304 | tf_op jit(solution)/shard_map/all_to_all | solution.py:550
  17.8 16.5 %collective-permute-start = (bf16[1056,128]{1,0:T(8,128)(2,1)}, bf16[1056,128]{1,0:T(8,128)(2,1)S(1)}, u32[]{:S(2)}, u32[]{:S(2)}) collective-permute-start(bf16[1056,128]{1,0:T(8,128)(2,1)} %get-tuple-element.26), channel_id=1, source_target_pairs={{0,2},{2,0},{4,6},{6,4},{8,10},{10,8},{12,14},{14,12},{16,18},{18,... | collective-permute-start | bytes 811016 | tf_op jit(solution)/shard_map/ppermute | solution.py:368
  18.1 27.7 %collective-permute-start.1 = (bf16[1056,128]{1,0:T(8,128)(2,1)}, bf16[1056,128]{1,0:T(8,128)(2,1)S(1)}, u32[]{:S(2)}, u32[]{:S(2)}) collective-permute-start(bf16[1056,128]{1,0:T(8,128)(2,1)} %get-tuple-element.31), channel_id=1, source_target_pairs={{0,4},{2,6},{4,0},{6,2},{8,12},{10,14},{12,8},{14,10},{16,20},{18,... | collective-permute-start | bytes 811016 | tf_op jit(solution)/shard_map/ppermute | solution.py:368
  19.2 26.5 %collective-permute-start.2 = (bf16[1056,128]{1,0:T(8,128)(2,1)}, bf16[1056,128]{1,0:T(8,128)(2,1)S(1)}, u32[]{:S(2)}, u32[]{:S(2)}) collective-permute-start(bf16[1056,128]{1,0:T(8,128)(2,1)} %get-tuple-element.32), channel_id=1, source_target_pairs={{0,6},{2,4},{4,2},{6,0},{8,14},{10,12},{12,10},{14,8},{16,22},{18,... | collective-permute-start | bytes 811016 | tf_op jit(solution)/shard_map/ppermute | solution.py:368
  34.3 11.5 %copy-start.2 = (bf16[1056,128]{1,0:T(8,128)(2,1)}, bf16[1056,128]{1,0:T(8,128)(2,1)S(1)}, u32[]{:S(2)}) copy-start(bf16[1056,128]{1,0:T(8,128)(2,1)S(1)} %collective-permute-done.refs_1_) | copy-start | bytes 811012
  45.8 0.7 copy-start.3
  45.8 0.8 copy-start.4
  48.8 40.4 %copy-start.11 = (s32[32,16]{0,1:T(8,128)S(1)}, s32[32,16]{0,1:T(8,128)}, u32[]{:S(2)}) copy-start(s32[32,16]{0,1:T(8,128)} %param.24) | copy-start | bytes 6148
  48.8 46.1 %copy-start.13 = (s32[32]{0:T(128)S(1)}, s32[32]{0:T(128)}, u32[]{:S(2)}) copy-start(s32[32]{0:T(128)} %param.25) | copy-start | bytes 388
  48.8 13.3 %collective-permute-start.5 = (bf16[1056,128]{1,0:T(8,128)(2,1)}, bf16[1056,128]{1,0:T(8,128)(2,1)S(1)}, u32[]{:S(2)}, u32[]{:S(2)}) collective-permute-start(bf16[1056,128]{1,0:T(8,128)(2,1)} %walk_states.2), channel_id=1, source_target_pairs={{0,8},{2,10},{4,12},{6,14},{8,16},{10,18},{12,20},{14,22},{16,24},... | collective-permute-start | bytes 811016 | tf_op jit(solution)/shard_map/ppermute | solution.py:375
  50.2 31.0 %collective-permute-start.4 = (bf16[1056,128]{1,0:T(8,128)(2,1)}, bf16[1056,128]{1,0:T(8,128)(2,1)S(1)}, u32[]{:S(2)}, u32[]{:S(2)}) collective-permute-start(bf16[1056,128]{1,0:T(8,128)(2,1)} %walk_states.2), channel_id=1, source_target_pairs={{0,16},{2,18},{4,20},{6,22},{8,24},{10,26},{12,28},{14,30},{1,17},... | collective-permute-start | bytes 811016 | tf_op jit(solution)/shard_map/ppermute | solution.py:375
  51.5 29.7 %collective-permute-start.3 = (bf16[1056,128]{1,0:T(8,128)(2,1)}, bf16[1056,128]{1,0:T(8,128)(2,1)S(1)}, u32[]{:S(2)}, u32[]{:S(2)}) collective-permute-start(bf16[1056,128]{1,0:T(8,128)(2,1)} %walk_states.2), channel_id=1, source_target_pairs={{0,24},{2,26},{4,28},{6,30},{1,25},{3,27},{5,29},{7,31}} | collective-permute-start | bytes 811016 | tf_op jit(solution)/shard_map/ppermute | solution.py:375
  62.1 27.1 %copy-start.5 = (bf16[1056,128]{1,0:T(8,128)(2,1)}, bf16[1056,128]{1,0:T(8,128)(2,1)S(1)}, u32[]{:S(2)}) copy-start(bf16[1056,128]{1,0:T(8,128)(2,1)S(1)} %collective-permute-done.5.refs_6_) | copy-start | bytes 811012
  81.2 8.0 %copy-start.6 = (bf16[1056,128]{1,0:T(8,128)(2,1)}, bf16[1056,128]{1,0:T(8,128)(2,1)S(1)}, u32[]{:S(2)}) copy-start(bf16[1056,128]{1,0:T(8,128)(2,1)S(1)} %collective-permute-done.4.refs_5_) | copy-start | bytes 811012
  81.2 8.1 %copy-start.7 = (bf16[1056,128]{1,0:T(8,128)(2,1)}, bf16[1056,128]{1,0:T(8,128)(2,1)S(1)}, u32[]{:S(2)}) copy-start(bf16[1056,128]{1,0:T(8,128)(2,1)S(1)} %collective-permute-done.3.refs_4_) | copy-start | bytes 811012
  81.2 1.4 copy-start.1
  82.6 85.4 %all-to-all-start.1 = ((bf16[16,2,128,256]{3,2,1,0:T(8,128)(2,1)}), bf16[16,2,128,256]{3,2,1,0:T(8,128)(2,1)S(1)}, u32[]{:S(2)}, u32[]{:S(2)}) async-start(bf16[16,2,128,256]{3,2,1,0:T(8,128)(2,1)} %pack.2), calls=%async_computation.1 | async-start | bytes 4194304 | tf_op jit(solution)/shard_map/all_to_all | solution.py:562
  92.2 57.5 %collective-permute-start.6 = (bf16[1024,128]{1,0:T(8,128)(2,1)}, bf16[1024,128]{1,0:T(8,128)(2,1)S(1)}, u32[]{:S(2)}, u32[]{:S(2)}) collective-permute-start(bf16[1024,128]{1,0:T(8,128)(2,1)} %get-tuple-element.39), channel_id=1, source_target_pairs={{0,2},{2,0},{4,6},{6,4},{8,10},{10,8},{12,14},{14,12},{16,18},{18,... | collective-permute-start | bytes 786440 | tf_op jit(solution)/shard_map/ppermute | solution.py:368
  92.4 57.2 %collective-permute-start.7 = (bf16[1024,128]{1,0:T(8,128)(2,1)}, bf16[1024,128]{1,0:T(8,128)(2,1)S(1)}, u32[]{:S(2)}, u32[]{:S(2)}) collective-permute-start(bf16[1024,128]{1,0:T(8,128)(2,1)} %get-tuple-element.40), channel_id=1, source_target_pairs={{0,4},{2,6},{4,0},{6,2},{8,12},{10,14},{12,8},{14,10},{16,20},{18,... | collective-permute-start | bytes 786440 | tf_op jit(solution)/shard_map/ppermute | solution.py:368
  93.6 56.1 %collective-permute-start.8 = (bf16[1024,128]{1,0:T(8,128)(2,1)}, bf16[1024,128]{1,0:T(8,128)(2,1)S(1)}, u32[]{:S(2)}, u32[]{:S(2)}) collective-permute-start(bf16[1024,128]{1,0:T(8,128)(2,1)} %get-tuple-element.41), channel_id=1, source_target_pairs={{0,6},{2,4},{4,2},{6,0},{8,14},{10,12},{12,10},{14,8},{16,22},{18,... | collective-permute-start | bytes 786440 | tf_op jit(solution)/shard_map/ppermute | solution.py:368
  149.7 0.7 copy-start.8
  149.7 0.8 copy-start.9
  149.7 0.8 copy-start.10
  157.7 4.3 %collective-permute-start.9 = (f32[8,256]{1,0:T(8,128)}, f32[8,256]{1,0:T(8,128)S(1)}, u32[]{:S(2)}, u32[]{:S(2)}) collective-permute-start(f32[8,256]{1,0:T(8,128)} %get-tuple-element.43.refs_0_), channel_id=1, source_target_pairs={{0,1},{1,0},{2,3},{3,2},{4,5},{5,4},{6,7},{7,6},{8,9},{9,8},{10,11... | collective-permute-start | bytes 24584 | tf_op jit(solution)/shard_map/ppermute | solution.py:589
  161.9 0.6 copy-start.12
  168.0 1.3 copy-start
